TPU v7x, 128 devices: a whole 4x4x4 slice. The times are simulated.
128 devices in a mesh: row: 8 (over x_lo, z), col: 16 (over y, x_hi, core).
Axes of the slice: x: 4 (x_hi: 2, x_lo: 2; x = x_hi * 2 + x_lo), y: 4, z: 4, core: 2. Of those that a mesh axis runs over, the one named last changes fastest.
Arguments:
- start_vectors: bfloat16 [65536, 512], P(('row', 'col')), may hold values from -6 to 6
- tiles: bfloat16 [512, 16, 2, 128, 128], P('row', 'col'), may hold values from -0.046875 to 0.046875
- tile_col: int32 [512, 16, 2], P('row', 'col'), may hold values from 0 to 31, as said below
- tile_count: int32 [512, 16], P('row', 'col'), may hold values from 1 to 2, as said below
Outputs:
- filtered: bfloat16 [65536, 512], P(('row', 'col'))
Inputs may be any that keep to these rules, and one draw needn't show every extreme that they name: `tile_col`: the 2 entries of one block row and one column group are distinct; every device's first block row uses local block columns 0 and 31. `tile_count`: every device's first block row has all 2 slots live in every column group.
All inputs are finite; a program needn't handle non-finite values.
Results may differ from a plain program's by a relative error of at most 0.019.
Values may be sent and summed in bfloat16 or wider, within the bound.
No kernel may reach another device: no remote copies, remote signals or barrier semaphores. Data moves between devices by JAX's collectives and lax.ppermute only.
A program may use at most 128 MiB of HBM per device.

v0:
```python
import functools

import jax
import jax.numpy as jnp
import numpy as np
from jax import lax
from jax.experimental import pallas as pl
from jax.experimental.pallas import tpu as pltpu
from jax.sharding import Mesh, PartitionSpec as P

DEGREE = 3
BLK = 128
LANES = 128
CHUNKS = 2
UNIT = 8


def flips(first):
    return [(2 * i + c, 2 * (i ^ (1 if (c == 0) == first else 3)) + c) for i in range(4) for c in range(2)]


def swap(x, axis):
    return lax.ppermute(x, axis, [(0, 1), (1, 0)])


def product_kernel(order, picks, own_a, own_b, other_a, other_b, *refs):
    *pieces, out, held = refs
    step = pl.program_id(0)

    @pl.when(step == 0)
    def _():
        at = 0
        for piece in pieces:
            held[pl.ds(at, piece.shape[0]), :] = piece[...]
            at += piece.shape[0]
        held[pl.ds(8 * UNIT * BLK, BLK), :] = jnp.zeros((BLK, LANES), held.dtype)

    for half, (own, other) in enumerate(((own_a, other_a), (own_b, other_b))):
        group = order[2 * step + half]
        for j in range(4):
            base = (group * 4 + j) * 4
            picked = jnp.concatenate(
                [held[pl.ds(pl.multiple_of(picks[base + k], BLK), BLK), :] for k in range(4)], axis=0
            )
            row = jnp.concatenate([own[j, 0], own[j, 1], other[j, 0], other[j, 1]], axis=1)
            total = jnp.dot(row, picked, preferred_element_type=jnp.float32)
            out[pl.ds((half * 4 + j) * BLK, BLK), :] = total.astype(out.dtype)


def products(order, picks, own, other, pieces):
    def tile_spec(half):
        return pl.BlockSpec((4, 2, BLK, BLK), lambda s, order, picks: (order[2 * s + half], 0, 0, 0))

    return pl.pallas_call(
        product_kernel,
        grid_spec=pltpu.PrefetchScalarGridSpec(
            num_scalar_prefetch=2,
            grid=(8,),
            in_specs=[tile_spec(0), tile_spec(1), tile_spec(0), tile_spec(1)] + [pl.BlockSpec(piece.shape, lambda s, order, picks: (0, 0)) for piece in pieces],
            out_specs=pl.BlockSpec((UNIT * BLK, LANES), lambda s, order, picks: (s, 0)),
            scratch_shapes=[pltpu.VMEM(((8 * UNIT + 1) * BLK, LANES), jnp.bfloat16)],
        ),
        out_shape=jax.ShapeDtypeStruct((8 * UNIT * BLK, LANES), jnp.bfloat16),
        compiler_params=pltpu.CompilerParams(vmem_limit_bytes=24 << 20),
        cost_estimate=pl.CostEstimate(flops=64 * 2 * 128 * 512 * 128, bytes_accessed=12 << 20, transcendentals=0),
        name="products",
    )(order, picks, own, own, other, other, *pieces)


def add(*terms):
    total = terms[0].astype(jnp.float32)
    for term in terms[1:]:
        total = total + term.astype(jnp.float32)
    return total


def body(start_vectors, tiles, tile_col, tile_count):
    xl, z, y, xh, c = (lax.axis_index(a) for a in ("xl", "z", "y", "xh", "c"))
    rows = start_vectors.shape[0]
    half = start_vectors.shape[1] // 2

    mine = lax.dynamic_slice(start_vectors, (0, c * half), (rows, half))
    theirs = swap(lax.dynamic_slice(start_vectors, (0, (1 - c) * half), (rows, half)), "c")
    first = [
        jnp.concatenate([part[:, i * LANES : (i + 1) * LANES] for part in (mine, theirs)], axis=0)
        for i in range(CHUNKS)
    ]

    own = tiles[:, 0]
    other = swap(own, "c")

    r, i = tile_col[:, 0] // 4, tile_col[:, 0] % 4
    dx, dz = (r // 4) ^ xl, (r & 3) ^ z
    live = jnp.arange(2, dtype=jnp.int32)[None, :] < tile_count

    def code(core, shift):
        slot = jnp.where(dz == 0, 0, jnp.where(dz == 2, 3, jnp.where(dz == 1 + 2 * core, 1, 2)))
        return jnp.where(live, (slot * 2 + dx) * UNIT + shift + i, 8 * UNIT) * BLK

    picks = jnp.concatenate([code(c, 0), swap(code(1 - c, 4), "c")], axis=1).reshape(-1)

    far, near = 3 - 2 * c, 1 + 2 * c
    dy = jnp.stack([far, far, jnp.int32(2), jnp.int32(2), near, near, jnp.int32(0), jnp.int32(0)])
    unit = (y ^ dy) * 2 + (xh ^ np.array([1, 0] * 4, np.int32))
    order = ((unit * 2)[:, None] + (c ^ np.array([[0, 1]], np.int32))).reshape(-1).astype(jnp.int32)

    def gather(v):
        pair = jnp.concatenate([v, swap(v, "xl")], axis=0)
        side = lax.ppermute(pair, ("z", "c"), flips(True))
        rest = lax.ppermute(jnp.concatenate([pair, side], axis=0), ("z", "c"), flips(False))
        return pair, side, rest

    def scatter(p):
        u = UNIT * BLK
        one = lax.ppermute(p[: 4 * u], ("y", "c"), flips(False))
        two = lax.ppermute(add(p[4 * u : 6 * u], one[2 * u :]).astype(p.dtype), ("y", "c"), flips(True))
        three = swap(add(p[6 * u : 7 * u], one[:u], two[:u]).astype(p.dtype), "xh")
        return add(p[7 * u :], one[u : 2 * u], two[u:], three)

    previous, current = [None] * CHUNKS, first
    for degree in range(DEGREE):
        following = []
        for k in range(CHUNKS):
            total = scatter(products(order, picks, own, other, gather(current[k])))
            if degree:
                total = 2.0 * total - previous[k].astype(jnp.float32)
            following.append(total.astype(jnp.bfloat16))
        previous, current = current, following

    kept = jnp.concatenate([v[:rows] for v in current], axis=1)
    got = swap(jnp.concatenate([v[rows:] for v in current], axis=1), "c")
    return jnp.where(c == 0, jnp.concatenate([kept, got], axis=1), jnp.concatenate([got, kept], axis=1))


def solution(mesh):
    axes = ("xl", "z", "y", "xh", "c")
    fine = Mesh(mesh.devices.reshape(2, 4, 4, 2, 2), axes)
    row, col = axes[:2], axes[2:]
    placed = (
        P(axes, None),
        P(row, col, None, None, None),
        P(row, col, None),
        P(row, col),
    )
    return jax.shard_map(body, mesh=fine, in_specs=placed, out_specs=P(axes, None), check_vma=False)
```

profile of v0, /device:TPU:1, one launch (start us, length us, event | category | flops | bytes accessed | tf_op | source)
XLA Modules:
  0.0 308.5 jit_solution(9112674282780896624)
XLA Ops:
  3.5 5.1 %collective-permute-done.2 = bf16[512,256]{1,0:T(8,128)(2,1)S(1)} collective-permute-done((bf16[512,256]{1,0:T(8,128)(2,1)S(1)}, bf16[512,256]{1,0:T(8,128)(2,1)S(1)}, u32[]{:S(2)}, u32[]{:S(2)}) %collective-permute-start.2) | collective-permute-done | bytes 262176 | tf_op jit(solution)/shard_map/ppermute | solution.py:23
  10.0 6.2 %collective-permute-done.3 = bf16[1024,128]{1,0:T(8,128)(2,1)S(1)} collective-permute-done((bf16[1024,128]{1,0:T(8,128)(2,1)S(1)}, bf16[1024,128]{1,0:T(8,128)(2,1)S(1)}, u32[]{:S(2)}, u32[]{:S(2)}) %collective-permute-start.3) | collective-permute-done | bytes 262176 | tf_op jit(solution)/shard_map/ppermute | solution.py:23
  21.8 6.5 %collective-permute-done.21 = bf16[1024,128]{1,0:T(8,128)(2,1)S(1)} collective-permute-done((bf16[1024,128]{1,0:T(8,128)(2,1)S(1)}, bf16[1024,128]{1,0:T(8,128)(2,1)S(1)}, u32[]{:S(2)}, u32[]{:S(2)}) %collective-permute-start.21) | collective-permute-done | bytes 262176 | tf_op jit(solution)/shard_map/ppermute | solution.py:23
  30.9 11.1 %collective-permute-done.22.refs_1_ = bf16[2048,128]{1,0:T(8,128)(2,1)S(1)} collective-permute-done((bf16[2048,128]{1,0:T(8,128)(2,1)S(1)}, bf16[2048,128]{1,0:T(8,128)(2,1)S(1)}, u32[]{:S(2)}, u32[]{:S(2)}) %collective-permute-start.22) | collective-permute-done | bytes 524320 | tf_op jit(solution)/shard_map/ppermute | solution.py:109
  45.4 4.2 %collective-permute-done.5.refs_2_ = bf16[4096,128]{1,0:T(8,128)(2,1)S(1)} collective-permute-done((bf16[4096,128]{1,0:T(8,128)(2,1)}, bf16[4096,128]{1,0:T(8,128)(2,1)S(1)}, u32[]{:S(2)}, u32[]{:S(2)}) %collective-permute-start.5) | collective-permute-done | bytes 1048608 | tf_op jit(solution)/shard_map/ppermute | solution.py:110
  51.7 7.2 %products.6 = bf16[8192,128]{1,0:T(8,128)(2,1)S(1)} custom-call(s32[16]{0:T(128)S(1)} %add.173.order, s32[256]{0:T(256)S(1)} %reshape.8.picks, bf16[64,2,128,128]{3,2,1,0:T(8,128)(2,1)S(1)} %bitcast.35, bf16[64,2,128,128]{3,2,1,0:T(8,128)(2,1)S(1)} %bitcast.36, bf16[64,2,128,128]{3,2,1,0:T(8,128)(2,1)} %collective-permute-done.1.other_a.other_b, ...), custom_call_target="tpu_custom_call" | custom-call | flops 1073741824 | bytes 12582912 | tf_op jit(solution)/shard_map/products/pallas_call | solution.py:54
  60.9 7.6 %products.9 = bf16[8192,128]{1,0:T(8,128)(2,1)S(1)} custom-call(s32[16]{0:T(128)S(1)} %add.173.order, s32[256]{0:T(256)S(1)} %reshape.8.picks, bf16[64,2,128,128]{3,2,1,0:T(8,128)(2,1)S(1)} %bitcast.37, bf16[64,2,128,128]{3,2,1,0:T(8,128)(2,1)S(1)} %bitcast.38, bf16[64,2,128,128]{3,2,1,0:T(8,128)(2,1)} %collective-permute-done.1.other_a.other_b, ...), custom_call_target="tpu_custom_call" | custom-call | flops 1073741824 | bytes 12582912 | tf_op jit(solution)/shard_map/products/pallas_call | solution.py:54
  76.0 13.2 %collective-permute-done.24 = bf16[4096,128]{1,0:T(8,128)(2,1)S(1)} collective-permute-done((bf16[4096,128]{1,0:T(8,128)(2,1)S(1)}, bf16[4096,128]{1,0:T(8,128)(2,1)S(1)}, u32[]{:S(2)}, u32[]{:S(2)}) %collective-permute-start.24) | collective-permute-done | bytes 1048608 | tf_op jit(solution)/shard_map/ppermute | solution.py:115
  107.2 3.9 %collective-permute-done.9 = bf16[1024,128]{1,0:T(8,128)(2,1)S(1)} collective-permute-done((bf16[1024,128]{1,0:T(8,128)(2,1)S(1)}, bf16[1024,128]{1,0:T(8,128)(2,1)S(1)}, u32[]{:S(2)}, u32[]{:S(2)}) %collective-permute-start.9) | collective-permute-done | bytes 262176 | tf_op jit(solution)/shard_map/ppermute | solution.py:23
  128.2 15.6 %collective-permute-done.11.refs_2_ = bf16[4096,128]{1,0:T(8,128)(2,1)S(1)} collective-permute-done((bf16[4096,128]{1,0:T(8,128)(2,1)S(1)}, bf16[4096,128]{1,0:T(8,128)(2,1)S(1)}, u32[]{:S(2)}, u32[]{:S(2)}) %collective-permute-start.11) | collective-permute-done | bytes 1048608 | tf_op jit(solution)/shard_map/ppermute | solution.py:110
  143.7 7.2 %products.7 = bf16[8192,128]{1,0:T(8,128)(2,1)S(1)} custom-call(s32[16]{0:T(128)S(1)} %add.173.order, s32[256]{0:T(256)S(1)} %reshape.8.picks, bf16[64,2,128,128]{3,2,1,0:T(8,128)(2,1)S(1)} %bitcast.39, bf16[64,2,128,128]{3,2,1,0:T(8,128)(2,1)S(1)} %bitcast.40, bf16[64,2,128,128]{3,2,1,0:T(8,128)(2,1)} %collective-permute-done.1.other_a.other_b, ...), custom_call_target="tpu_custom_call" | custom-call | flops 1073741824 | bytes 12582912 | tf_op jit(solution)/shard_map/products/pallas_call | solution.py:54
  155.0 7.2 %products.10 = bf16[8192,128]{1,0:T(8,128)(2,1)S(1)} custom-call(s32[16]{0:T(128)S(1)} %add.173.order, s32[256]{0:T(256)S(1)} %reshape.8.picks, bf16[64,2,128,128]{3,2,1,0:T(8,128)(2,1)S(1)} %bitcast.41, bf16[64,2,128,128]{3,2,1,0:T(8,128)(2,1)S(1)} %bitcast.42, bf16[64,2,128,128]{3,2,1,0:T(8,128)(2,1)} %collective-permute-done.1.other_a.other_b, ...), custom_call_target="tpu_custom_call" | custom-call | flops 1073741824 | bytes 12582912 | tf_op jit(solution)/shard_map/products/pallas_call | solution.py:54
  168.0 11.1 %collective-permute-done.30 = bf16[4096,128]{1,0:T(8,128)(2,1)S(1)} collective-permute-done((bf16[4096,128]{1,0:T(8,128)(2,1)S(1)}, bf16[4096,128]{1,0:T(8,128)(2,1)S(1)}, u32[]{:S(2)}, u32[]{:S(2)}) %collective-permute-start.30) | collective-permute-done | bytes 1048608 | tf_op jit(solution)/shard_map/ppermute | solution.py:115
  183.5 8.1 %collective-permute-done.31 = bf16[2048,128]{1,0:T(8,128)(2,1)S(1)} collective-permute-done((bf16[2048,128]{1,0:T(8,128)(2,1)S(1)}, bf16[2048,128]{1,0:T(8,128)(2,1)S(1)}, u32[]{:S(2)}, u32[]{:S(2)}) %collective-permute-start.31) | collective-permute-done | bytes 524320 | tf_op jit(solution)/shard_map/ppermute | solution.py:116
  193.8 6.5 %collective-permute-done.32 = bf16[1024,128]{1,0:T(8,128)(2,1)S(1)} collective-permute-done((bf16[1024,128]{1,0:T(8,128)(2,1)S(1)}, bf16[1024,128]{1,0:T(8,128)(2,1)S(1)}, u32[]{:S(2)}, u32[]{:S(2)}) %collective-permute-start.32) | collective-permute-done | bytes 262176 | tf_op jit(solution)/shard_map/ppermute | solution.py:23
  202.4 6.7 %collective-permute-done.33 = bf16[1024,128]{1,0:T(8,128)(2,1)S(1)} collective-permute-done((bf16[1024,128]{1,0:T(8,128)(2,1)S(1)}, bf16[1024,128]{1,0:T(8,128)(2,1)S(1)}, u32[]{:S(2)}, u32[]{:S(2)}) %collective-permute-start.33) | collective-permute-done | bytes 262176 | tf_op jit(solution)/shard_map/ppermute | solution.py:23
  211.8 6.7 %collective-permute-done.34.refs_1_ = bf16[2048,128]{1,0:T(8,128)(2,1)S(1)} collective-permute-done((bf16[2048,128]{1,0:T(8,128)(2,1)S(1)}, bf16[2048,128]{1,0:T(8,128)(2,1)S(1)}, u32[]{:S(2)}, u32[]{:S(2)}) %collective-permute-start.34) | collective-permute-done | bytes 524320 | tf_op jit(solution)/shard_map/ppermute | solution.py:109
  218.7 17.9 %collective-permute-done.17.refs_2_ = bf16[4096,128]{1,0:T(8,128)(2,1)S(1)} collective-permute-done((bf16[4096,128]{1,0:T(8,128)(2,1)S(1)}, bf16[4096,128]{1,0:T(8,128)(2,1)S(1)}, u32[]{:S(2)}, u32[]{:S(2)}) %collective-permute-start.17) | collective-permute-done | bytes 1048608 | tf_op jit(solution)/shard_map/ppermute | solution.py:110
  236.6 7.2 %products.8 = bf16[8192,128]{1,0:T(8,128)(2,1)S(1)} custom-call(s32[16]{0:T(128)S(1)} %add.173.order, s32[256]{0:T(256)S(1)} %reshape.8.picks, bf16[64,2,128,128]{3,2,1,0:T(8,128)(2,1)S(1)} %bitcast.43, bf16[64,2,128,128]{3,2,1,0:T(8,128)(2,1)S(1)} %bitcast.44, bf16[64,2,128,128]{3,2,1,0:T(8,128)(2,1)} %collective-permute-done.1.other_a.other_b, ...), custom_call_target="tpu_custom_call" | custom-call | flops 1073741824 | bytes 12582912 | tf_op jit(solution)/shard_map/products/pallas_call | solution.py:54
  243.9 4.2 %collective-permute-done.35.refs_2_ = bf16[4096,128]{1,0:T(8,128)(2,1)S(1)} collective-permute-done((bf16[4096,128]{1,0:T(8,128)(2,1)S(1)}, bf16[4096,128]{1,0:T(8,128)(2,1)S(1)}, u32[]{:S(2)}, u32[]{:S(2)}) %collective-permute-start.35) | collective-permute-done | bytes 1048608 | tf_op jit(solution)/shard_map/ppermute | solution.py:110
  248.2 7.2 %products.11 = bf16[8192,128]{1,0:T(8,128)(2,1)S(1)} custom-call(s32[16]{0:T(128)S(1)} %add.173.order, s32[256]{0:T(256)S(1)} %reshape.8.picks, bf16[64,2,128,128]{3,2,1,0:T(8,128)(2,1)S(1)} %bitcast.45, bf16[64,2,128,128]{3,2,1,0:T(8,128)(2,1)S(1)} %bitcast.46, bf16[64,2,128,128]{3,2,1,0:T(8,128)(2,1)} %collective-permute-done.1.other_a.other_b, ...), custom_call_target="tpu_custom_call" | custom-call | flops 1073741824 | bytes 12582912 | tf_op jit(solution)/shard_map/products/pallas_call | solution.py:54
  261.1 8.4 %collective-permute-done.36 = bf16[4096,128]{1,0:T(8,128)(2,1)S(1)} collective-permute-done((bf16[4096,128]{1,0:T(8,128)(2,1)S(1)}, bf16[4096,128]{1,0:T(8,128)(2,1)S(1)}, u32[]{:S(2)}, u32[]{:S(2)}) %collective-permute-start.36) | collective-permute-done | bytes 1048608 | tf_op jit(solution)/shard_map/ppermute | solution.py:115
  277.1 8.1 %collective-permute-done.37 = bf16[2048,128]{1,0:T(8,128)(2,1)S(1)} collective-permute-done((bf16[2048,128]{1,0:T(8,128)(2,1)S(1)}, bf16[2048,128]{1,0:T(8,128)(2,1)S(1)}, u32[]{:S(2)}, u32[]{:S(2)}) %collective-permute-start.37) | collective-permute-done | bytes 524320 | tf_op jit(solution)/shard_map/ppermute | solution.py:116
  292.5 13.8 %collective-permute-start.39 = (bf16[512,256]{1,0:T(8,128)(2,1)S(1)}, bf16[512,256]{1,0:T(8,128)(2,1)S(1)}, u32[]{:S(2)}, u32[]{:S(2)}) collective-permute-start(bf16[512,256]{1,0:T(8,128)(2,1)S(1)} %pad_maximum_fusion.14), channel_id=1, source_target_pairs={{0,1},{1,0},{2,3},{3,2},{4,5},{5,4},{6,7},{7,6},{8,9},{9,8},{10,11... | collective-permute-start | bytes 786440 | tf_op jit(solution)/shard_map/ppermute | solution.py:23
  (134 shorter events, 107.0 us)
Async XLA Ops:
  0.0 49.5 %collective-permute-start.1 = (bf16[64,2,128,128]{3,2,1,0:T(8,128)(2,1)}, bf16[64,2,128,128]{3,2,1,0:T(8,128)(2,1)}, u32[]{:S(2)}, u32[]{:S(2)}) collective-permute-start(bf16[64,2,128,128]{3,2,1,0:T(8,128)(2,1)} %bitcast.34), channel_id=1, source_target_pairs={{0,1},{1,0},{2,3},{3,2},{4,5},{5,4},{6,7},{7,6},{8,9},{9,8},{10,11... | collective-permute-start | bytes 12582920 | tf_op jit(solution)/shard_map/ppermute | solution.py:23
  16.3 12.8 %collective-permute-start.4 = (bf16[2048,128]{1,0:T(8,128)(2,1)S(1)}, bf16[2048,128]{1,0:T(8,128)(2,1)S(1)}, u32[]{:S(2)}, u32[]{:S(2)}) collective-permute-start(bf16[2048,128]{1,0:T(8,128)(2,1)S(1)} %pad_maximum_fusion.6.refs_0_), channel_id=1, source_target_pairs={{0,16},{1,49},{16,0},{17,33},{32,48},{33,17},{48,32},{49,1},{2,18}... | collective-permute-start | bytes 1572872 | tf_op jit(solution)/shard_map/ppermute | solution.py:109
  21.5 21.6 %collective-permute-start = (s32[64,2]{0,1:T(2,128)S(1)}, s32[64,2]{0,1:T(2,128)}, u32[]{:S(2)}, u32[]{:S(2)}) collective-permute-start(s32[64,2]{0,1:T(2,128)S(1)} %get-tuple-element.14), channel_id=1, source_target_pairs={{0,1},{1,0},{2,3},{3,2},{4,5},{5,4},{6,7},{7,6},{8,9},{9,8},{10,11... | collective-permute-start | bytes 1544 | tf_op jit(solution)/shard_map/ppermute | solution.py:23
  29.0 12.9 %collective-permute-start.22 = (bf16[2048,128]{1,0:T(8,128)(2,1)S(1)}, bf16[2048,128]{1,0:T(8,128)(2,1)S(1)}, u32[]{:S(2)}, u32[]{:S(2)}) collective-permute-start(bf16[2048,128]{1,0:T(8,128)(2,1)S(1)} %pad_maximum_fusion.9.refs_0_), channel_id=1, source_target_pairs={{0,16},{1,49},{16,0},{17,33},{32,48},{33,17},{48,32},{49,1},{2,18}... | collective-permute-start | bytes 1572872 | tf_op jit(solution)/shard_map/ppermute | solution.py:109
  30.2 19.3 %collective-permute-start.5 = (bf16[4096,128]{1,0:T(8,128)(2,1)}, bf16[4096,128]{1,0:T(8,128)(2,1)S(1)}, u32[]{:S(2)}, u32[]{:S(2)}) collective-permute-start(bf16[4096,128]{1,0:T(8,128)(2,1)} %pad_maximum_fusion), channel_id=1, source_target_pairs={{0,48},{1,17},{16,32},{17,1},{32,16},{33,49},{48,0},{49,33},{2,50}... | collective-permute-start | bytes 3145736 | tf_op jit(solution)/shard_map/ppermute | solution.py:110
  43.0 17.9 %collective-permute-start.23 = (bf16[4096,128]{1,0:T(8,128)(2,1)}, bf16[4096,128]{1,0:T(8,128)(2,1)}, u32[]{:S(2)}, u32[]{:S(2)}) collective-permute-start(bf16[4096,128]{1,0:T(8,128)(2,1)} %pad_maximum_fusion.3), channel_id=1, source_target_pairs={{0,48},{1,17},{16,32},{17,1},{32,16},{33,49},{48,0},{49,33},{2,50}... | collective-permute-start | bytes 3145736 | tf_op jit(solution)/shard_map/ppermute | solution.py:110
  59.0 14.0 %collective-permute-start.6 = (bf16[4096,128]{1,0:T(8,128)(2,1)S(1)}, bf16[4096,128]{1,0:T(8,128)(2,1)S(1)}, u32[]{:S(2)}, u32[]{:S(2)}) collective-permute-start(bf16[4096,128]{1,0:T(8,128)(2,1)S(1)} %slice.250), channel_id=1, source_target_pairs={{0,12},{1,5},{4,8},{5,1},{8,4},{9,13},{12,0},{13,9},{2,14},{3,7},{... | collective-permute-start | bytes 3145736 | tf_op jit(solution)/shard_map/ppermute | solution.py:115
  68.6 20.7 %collective-permute-start.24 = (bf16[4096,128]{1,0:T(8,128)(2,1)S(1)}, bf16[4096,128]{1,0:T(8,128)(2,1)S(1)}, u32[]{:S(2)}, u32[]{:S(2)}) collective-permute-start(bf16[4096,128]{1,0:T(8,128)(2,1)S(1)} %slice.279), channel_id=1, source_target_pairs={{0,12},{1,5},{4,8},{5,1},{8,4},{9,13},{12,0},{13,9},{2,14},{3,7},{... | collective-permute-start | bytes 3145736 | tf_op jit(solution)/shard_map/ppermute | solution.py:115
  73.2 19.0 %collective-permute-start.7 = (bf16[2048,128]{1,0:T(8,128)(2,1)S(1)}, bf16[2048,128]{1,0:T(8,128)(2,1)S(1)}, u32[]{:S(2)}, u32[]{:S(2)}) collective-permute-start(bf16[2048,128]{1,0:T(8,128)(2,1)S(1)} %add_convert_fusion.5), channel_id=1, source_target_pairs={{0,4},{1,13},{4,0},{5,9},{8,12},{9,5},{12,8},{13,1},{2,6},{3,15},{... | collective-permute-start | bytes 1572872 | tf_op jit(solution)/shard_map/ppermute | solution.py:116
  120.6 23.1 %collective-permute-start.11 = (bf16[4096,128]{1,0:T(8,128)(2,1)S(1)}, bf16[4096,128]{1,0:T(8,128)(2,1)S(1)}, u32[]{:S(2)}, u32[]{:S(2)}) collective-permute-start(bf16[4096,128]{1,0:T(8,128)(2,1)S(1)} %pad_maximum_fusion.1), channel_id=1, source_target_pairs={{0,48},{1,17},{16,32},{17,1},{32,16},{33,49},{48,0},{49,33},{2,50}... | collective-permute-start | bytes 3145736 | tf_op jit(solution)/shard_map/ppermute | solution.py:110
  126.2 28.7 %collective-permute-start.29 = (bf16[4096,128]{1,0:T(8,128)(2,1)S(1)}, bf16[4096,128]{1,0:T(8,128)(2,1)S(1)}, u32[]{:S(2)}, u32[]{:S(2)}) collective-permute-start(bf16[4096,128]{1,0:T(8,128)(2,1)S(1)} %pad_maximum_fusion.4), channel_id=1, source_target_pairs={{0,48},{1,17},{16,32},{17,1},{32,16},{33,49},{48,0},{49,33},{2,50}... | collective-permute-start | bytes 3145736 | tf_op jit(solution)/shard_map/ppermute | solution.py:110
  151.0 14.0 %collective-permute-start.12 = (bf16[4096,128]{1,0:T(8,128)(2,1)S(1)}, bf16[4096,128]{1,0:T(8,128)(2,1)S(1)}, u32[]{:S(2)}, u32[]{:S(2)}) collective-permute-start(bf16[4096,128]{1,0:T(8,128)(2,1)S(1)} %slice.259), channel_id=1, source_target_pairs={{0,12},{1,5},{4,8},{5,1},{8,4},{9,13},{12,0},{13,9},{2,14},{3,7},{... | collective-permute-start | bytes 3145736 | tf_op jit(solution)/shard_map/ppermute | solution.py:115
  162.3 16.8 %collective-permute-start.30 = (bf16[4096,128]{1,0:T(8,128)(2,1)S(1)}, bf16[4096,128]{1,0:T(8,128)(2,1)S(1)}, u32[]{:S(2)}, u32[]{:S(2)}) collective-permute-start(bf16[4096,128]{1,0:T(8,128)(2,1)S(1)} %slice.288), channel_id=1, source_target_pairs={{0,12},{1,5},{4,8},{5,1},{8,4},{9,13},{12,0},{13,9},{2,14},{3,7},{... | collective-permute-start | bytes 3145736 | tf_op jit(solution)/shard_map/ppermute | solution.py:115
  165.2 16.6 %collective-permute-start.13 = (bf16[2048,128]{1,0:T(8,128)(2,1)S(1)}, bf16[2048,128]{1,0:T(8,128)(2,1)S(1)}, u32[]{:S(2)}, u32[]{:S(2)}) collective-permute-start(bf16[2048,128]{1,0:T(8,128)(2,1)S(1)} %add_convert_fusion.4), channel_id=1, source_target_pairs={{0,4},{1,13},{4,0},{5,9},{8,12},{9,5},{12,8},{13,1},{2,6},{3,15},{... | collective-permute-start | bytes 1572872 | tf_op jit(solution)/shard_map/ppermute | solution.py:116
  179.2 12.4 %collective-permute-start.31 = (bf16[2048,128]{1,0:T(8,128)(2,1)S(1)}, bf16[2048,128]{1,0:T(8,128)(2,1)S(1)}, u32[]{:S(2)}, u32[]{:S(2)}) collective-permute-start(bf16[2048,128]{1,0:T(8,128)(2,1)S(1)} %add_convert_fusion.1), channel_id=1, source_target_pairs={{0,4},{1,13},{4,0},{5,9},{8,12},{9,5},{12,8},{13,1},{2,6},{3,15},{... | collective-permute-start | bytes 1572872 | tf_op jit(solution)/shard_map/ppermute | solution.py:116
  181.9 11.6 %collective-permute-start.14 = (bf16[1024,128]{1,0:T(8,128)(2,1)S(1)}, bf16[1024,128]{1,0:T(8,128)(2,1)S(1)}, u32[]{:S(2)}, u32[]{:S(2)}) collective-permute-start(bf16[1024,128]{1,0:T(8,128)(2,1)S(1)} %add_convert_fusion.11), channel_id=1, source_target_pairs={{0,2},{2,0},{1,3},{3,1},{4,6},{6,4},{5,7},{7,5},{8,10},{10,8},{9,1... | collective-permute-start | bytes 786440 | tf_op jit(solution)/shard_map/ppermute | solution.py:23
  211.7 24.9 %collective-permute-start.17 = (bf16[4096,128]{1,0:T(8,128)(2,1)S(1)}, bf16[4096,128]{1,0:T(8,128)(2,1)S(1)}, u32[]{:S(2)}, u32[]{:S(2)}) collective-permute-start(bf16[4096,128]{1,0:T(8,128)(2,1)S(1)} %pad_maximum_fusion.2), channel_id=1, source_target_pairs={{0,48},{1,17},{16,32},{17,1},{32,16},{33,49},{48,0},{49,33},{2,50}... | collective-permute-start | bytes 3145736 | tf_op jit(solution)/shard_map/ppermute | solution.py:110
  218.6 29.6 %collective-permute-start.35 = (bf16[4096,128]{1,0:T(8,128)(2,1)S(1)}, bf16[4096,128]{1,0:T(8,128)(2,1)S(1)}, u32[]{:S(2)}, u32[]{:S(2)}) collective-permute-start(bf16[4096,128]{1,0:T(8,128)(2,1)S(1)} %pad_maximum_fusion.5), channel_id=1, source_target_pairs={{0,48},{1,17},{16,32},{17,1},{32,16},{33,49},{48,0},{49,33},{2,50}... | collective-permute-start | bytes 3145736 | tf_op jit(solution)/shard_map/ppermute | solution.py:110
  243.8 14.0 %collective-permute-start.18 = (bf16[4096,128]{1,0:T(8,128)(2,1)S(1)}, bf16[4096,128]{1,0:T(8,128)(2,1)S(1)}, u32[]{:S(2)}, u32[]{:S(2)}) collective-permute-start(bf16[4096,128]{1,0:T(8,128)(2,1)S(1)} %slice.268), channel_id=1, source_target_pairs={{0,12},{1,5},{4,8},{5,1},{8,4},{9,13},{12,0},{13,9},{2,14},{3,7},{... | collective-permute-start | bytes 3145736 | tf_op jit(solution)/shard_map/ppermute | solution.py:115
  255.5 14.0 %collective-permute-start.36 = (bf16[4096,128]{1,0:T(8,128)(2,1)S(1)}, bf16[4096,128]{1,0:T(8,128)(2,1)S(1)}, u32[]{:S(2)}, u32[]{:S(2)}) collective-permute-start(bf16[4096,128]{1,0:T(8,128)(2,1)S(1)} %slice.297), channel_id=1, source_target_pairs={{0,12},{1,5},{4,8},{5,1},{8,4},{9,13},{12,0},{13,9},{2,14},{3,7},{... | collective-permute-start | bytes 3145736 | tf_op jit(solution)/shard_map/ppermute | solution.py:115
  258.0 15.6 %collective-permute-start.19 = (bf16[2048,128]{1,0:T(8,128)(2,1)S(1)}, bf16[2048,128]{1,0:T(8,128)(2,1)S(1)}, u32[]{:S(2)}, u32[]{:S(2)}) collective-permute-start(bf16[2048,128]{1,0:T(8,128)(2,1)S(1)} %add_convert_fusion.3), channel_id=1, source_target_pairs={{0,4},{1,13},{4,0},{5,9},{8,12},{9,5},{12,8},{13,1},{2,6},{3,15},{... | collective-permute-start | bytes 1572872 | tf_op jit(solution)/shard_map/ppermute | solution.py:116
  269.6 15.6 %collective-permute-start.37 = (bf16[2048,128]{1,0:T(8,128)(2,1)S(1)}, bf16[2048,128]{1,0:T(8,128)(2,1)S(1)}, u32[]{:S(2)}, u32[]{:S(2)}) collective-permute-start(bf16[2048,128]{1,0:T(8,128)(2,1)S(1)} %add_convert_fusion), channel_id=1, source_target_pairs={{0,4},{1,13},{4,0},{5,9},{8,12},{9,5},{12,8},{13,1},{2,6},{3,15},{... | collective-permute-start | bytes 1572872 | tf_op jit(solution)/shard_map/ppermute | solution.py:116
  273.7 14.8 %collective-permute-start.20 = (bf16[1024,128]{1,0:T(8,128)(2,1)S(1)}, bf16[1024,128]{1,0:T(8,128)(2,1)S(1)}, u32[]{:S(2)}, u32[]{:S(2)}) collective-permute-start(bf16[1024,128]{1,0:T(8,128)(2,1)S(1)} %add_convert_fusion.10), channel_id=1, source_target_pairs={{0,2},{2,0},{1,3},{3,1},{4,6},{6,4},{5,7},{7,5},{8,10},{10,8},{9,1... | collective-permute-start | bytes 786440 | tf_op jit(solution)/shard_map/ppermute | solution.py:23
  292.5 14.9 %collective-permute-start.39 = (bf16[512,256]{1,0:T(8,128)(2,1)S(1)}, bf16[512,256]{1,0:T(8,128)(2,1)S(1)}, u32[]{:S(2)}, u32[]{:S(2)}) collective-permute-start(bf16[512,256]{1,0:T(8,128)(2,1)S(1)} %pad_maximum_fusion.14), channel_id=1, source_target_pairs={{0,1},{1,0},{2,3},{3,2},{4,5},{5,4},{6,7},{7,6},{8,9},{9,8},{10,11... | collective-permute-start | bytes 786440 | tf_op jit(solution)/shard_map/ppermute | solution.py:23
  (24 other events, 259.4 us)
where the time goes:
time: 309 us; the launch traced here: 308 us
  waiting for transfers between devices  180 us (58%)
  starting transfers between devices  70.1 us (23%)
  Pallas kernels  43.6 us (14%)
  other arithmetic  7.58 us (2%)
  local copies, waits for them, and re-layouts  7.09 us (2%)
    ppermute x16, waiting for transfers between devices, swap(): return lax.ppermute(x, axis, [(0, 1), (1, 0)])  47 us
    ppermute x6, waiting for transfers between devices, gather(): lax.ppermute(jnp.concatenate([pair, side], axis=0), ('z', 'c'), flips(Fal...  45.5 us
    pallas_call x6, Pallas kernels, products(): pl.pallas_call(product_kernel, grid_spec=pltpu.PrefetchScalarGridSpec(num...  43.6 us
    ppermute x6, waiting for transfers between devices, scatter(): one = lax.ppermute(p[:4 * u], ('y', 'c'), flips(False))  40.2 us
    ppermute x16, starting transfers between devices, swap(): return lax.ppermute(x, axis, [(0, 1), (1, 0)])  37 us
    ppermute x6, waiting for transfers between devices, gather(): side = lax.ppermute(pair, ('z', 'c'), flips(True))  25.7 us
    ppermute x6, waiting for transfers between devices, scatter(): lax.ppermute(add(p[4 * u:6 * u], one[2 * u:]).astype(p.dtype), ('y', 'c')...  21.2 us
    ppermute x6, starting transfers between devices, scatter(): lax.ppermute(add(p[4 * u:6 * u], one[2 * u:]).astype(p.dtype), ('y', 'c')...  17.1 us
  transfers between devices with their start and end apart: 40, of which 31 were waited for; matrix products, arithmetic and copies ran while one was open for 3% of the time, Pallas kernels for 14%

commit v1 on v0

v1 whole, which is shorter than its diff:
```python
import functools

import jax
import jax.numpy as jnp
import numpy as np
from jax import lax
from jax.experimental import pallas as pl
from jax.experimental.pallas import tpu as pltpu
from jax.sharding import Mesh, PartitionSpec as P

DEGREE = 3
BLK = 128
CHUNKS = (96, 80, 80)
TURNS = (0, 0, 0, 1, 2, 1, 0, 2, 1, 2, 0, 1, 0, 2, 0, 1, 0, 2, 1, 0, 2, 1, 2, 1, 0, 2, 1, 2, 0, 1, 0, 2, 0, 1, 0, 2, 1, 0, 2, 1, 2, 1, 0, 2, 1, 2, 0, 1, 0, 2, 1, 2, 1, 2)
UNIT = 8


def flips(first):
    return [(2 * i + c, 2 * (i ^ (1 if (c == 0) == first else 3)) + c) for i in range(4) for c in range(2)]


def swap(x, axis):
    return lax.ppermute(x, axis, [(0, 1), (1, 0)])


def product_kernel(order, picks, merged, *refs):
    *pieces, out, held = refs
    step = pl.program_id(0)
    size = held.shape[0] // (8 * UNIT + 1)

    @pl.when(step == 0)
    def _():
        at = 0
        for piece in pieces:
            held[pl.ds(at, piece.shape[0]), :] = piece[...]
            at += piece.shape[0]
        held[pl.ds(at, size), :] = jnp.zeros((size, BLK), held.dtype)

    for half in range(2):
        group = order[2 * step + half]
        for j in range(4):
            a = group * 4 + j
            picked = jnp.concatenate(
                [held[pl.ds(pl.multiple_of(picks[a * 4 + k] * size, 16), size), :] for k in range(4)], axis=1
            )
            total = lax.dot_general(picked, merged[a], (((1,), (1,)), ((), ())), preferred_element_type=jnp.float32)
            at = pl.multiple_of((step * UNIT + half * 4 + j) * size, 16)
            out[pl.ds(at, size), :] = total.astype(out.dtype)


def products(order, picks, merged, pieces):
    rows = sum(piece.shape[0] for piece in pieces)
    whole = pl.BlockSpec(memory_space=pltpu.VMEM)
    return pl.pallas_call(
        product_kernel,
        grid_spec=pltpu.PrefetchScalarGridSpec(
            num_scalar_prefetch=2,
            grid=(8,),
            in_specs=[whole] * (1 + len(pieces)),
            out_specs=whole,
            scratch_shapes=[pltpu.VMEM((rows + rows // (8 * UNIT), BLK), jnp.bfloat16)],
        ),
        out_shape=jax.ShapeDtypeStruct((rows, BLK), jnp.bfloat16),
        compiler_params=pltpu.CompilerParams(vmem_limit_bytes=24 << 20),
        cost_estimate=pl.CostEstimate(flops=2 * rows * 512 * 128, bytes_accessed=4 << 20, transcendentals=0),
        name="products",
    )(order, picks, merged, *pieces)


def add(*terms):
    total = terms[0].astype(jnp.float32)
    for term in terms[1:]:
        total = total + term.astype(jnp.float32)
    return total


def body(start_vectors, tiles, tile_col, tile_count):
    xl, z, y, xh, c = (lax.axis_index(a) for a in ("xl", "z", "y", "xh", "c"))
    rows = start_vectors.shape[0]
    half = start_vectors.shape[1] // 2

    turned = start_vectors.reshape(rows // BLK, BLK, 2 * half).transpose(0, 2, 1)
    mine = lax.dynamic_slice(turned, (0, c * half, 0), (rows // BLK, half, BLK))
    theirs = swap(lax.dynamic_slice(turned, (0, (1 - c) * half, 0), (rows // BLK, half, BLK)), "c")
    both = jnp.concatenate([mine, theirs], axis=0)
    edges = np.cumsum((0,) + CHUNKS)
    first = [both[:, i:j].reshape(-1, BLK) for i, j in zip(edges[:-1], edges[1:])]

    own = tiles[:, 0]
    own, first = lax.optimization_barrier((own, first))
    other = swap(own, "c")
    merged = jnp.concatenate([own[:, 0], own[:, 1], other[:, 0], other[:, 1]], axis=2)

    r, i = tile_col[:, 0] // 4, tile_col[:, 0] % 4
    dx, dz = (r // 4) ^ xl, (r & 3) ^ z
    live = jnp.arange(2, dtype=jnp.int32)[None, :] < tile_count

    def code(core, shift):
        slot = jnp.where(dz == 0, 0, jnp.where(dz == 2, 3, jnp.where(dz == 1 + 2 * core, 1, 2)))
        return jnp.where(live, (slot * 2 + dx) * UNIT + shift + i, 8 * UNIT)

    picks = jnp.concatenate([code(c, 0), swap(code(1 - c, 4), "c")], axis=1).reshape(-1)

    far, near = 3 - 2 * c, 1 + 2 * c
    dy = jnp.stack([far, far, jnp.int32(2), jnp.int32(2), near, near, jnp.int32(0), jnp.int32(0)])
    unit = (y ^ dy) * 2 + (xh ^ np.array([1, 0] * 4, np.int32))
    order = ((unit * 2)[:, None] + (c ^ np.array([[0, 1]], np.int32))).reshape(-1).astype(jnp.int32)

    def chain(v):
        previous = None
        u = v.shape[0]
        for degree in range(DEGREE):
            v = yield v
            pair = jnp.concatenate([v, swap(v, "xl")], axis=0)
            pair = yield pair
            side = lax.ppermute(pair, ("z", "c"), flips(True))
            four = yield jnp.concatenate([pair, side], axis=0)
            rest = lax.ppermute(four, ("z", "c"), flips(False))
            p = yield products(order, picks, merged, (four, rest))
            one = lax.ppermute(p[: 4 * u], ("y", "c"), flips(False))
            sent = yield add(p[4 * u : 6 * u], one[2 * u :]).astype(p.dtype)
            two = lax.ppermute(sent, ("y", "c"), flips(True))
            sent = yield add(p[6 * u : 7 * u], one[:u], two[:u]).astype(p.dtype)
            three = swap(sent, "xh")
            total = add(p[7 * u :], one[u : 2 * u], two[u:], three)
            if degree:
                total = 2.0 * total - previous.astype(jnp.float32)
            previous, v = v, total.astype(v.dtype)
        yield v

    chains = [chain(v) for v in first]
    waiting = [next(steps) for steps in chains]
    last = None
    for k in TURNS:
        if last is None:
            last = waiting[k]
        else:
            last, _ = lax.optimization_barrier((waiting[k], last))
        waiting[k] = chains[k].send(last)

    done = jnp.concatenate([v.reshape(2 * rows // BLK, -1, BLK) for v in waiting], axis=1)
    kept, got = done[: rows // BLK], swap(done[rows // BLK :], "c")
    turned = jnp.where(c == 0, jnp.concatenate([kept, got], axis=1), jnp.concatenate([got, kept], axis=1))
    return turned.transpose(0, 2, 1).reshape(rows, 2 * half)


def solution(mesh):
    axes = ("xl", "z", "y", "xh", "c")
    fine = Mesh(mesh.devices.reshape(2, 4, 4, 2, 2), axes)
    row, col = axes[:2], axes[2:]
    placed = (
        P(axes, None),
        P(row, col, None, None, None),
        P(row, col, None),
        P(row, col),
    )
    return jax.shard_map(body, mesh=fine, in_specs=placed, out_specs=P(axes, None), check_vma=False)
```

time: 309 us -> 257 us (0.83)
  waiting for transfers between devices: 180 us -> 96.7 us
  starting transfers between devices: 70.1 us -> 100 us
  local copies, waits for them, and re-layouts: 7.09 us -> 13.9 us
    ppermute x24 -> x36, waiting for transfers between devices: 133 us -> 71.9 us  [the longest x9 28 us: chain(): two = lax.ppermute(sent, ('y', 'c'), flips(True))]
    ppermute x24 -> x36, starting transfers between devices: 33.2 us -> 65.5 us  [the longest x9 38.7 us: chain(): two = lax.ppermute(sent, ('y', 'c'), flips(True))]
    ppermute x16 -> x22, waiting for transfers between devices: 47 us -> 24.8 us  [swap(): return lax.ppermute(x, axis, [(0, 1), (1, 0)])]
    squeeze x0 -> x2, local copies, waits for them, and re-layouts: none -> 5.59 us  [the longest x1 2.8 us: body(): other[:, 0]]
    pallas_call x6 -> x9, Pallas kernels: 43.6 us -> 40.9 us  [products(): pl.pallas_call(product_kernel, grid_spec=pltpu.PrefetchScalarGridSpec(num...]
    ppermute x16 -> x22, starting transfers between devices: 37 us -> 34.7 us  [swap(): return lax.ppermute(x, axis, [(0, 1), (1, 0)])]
  transfers between devices with their start and end apart: 40 -> 58, of which waited for: 31 -> 32; matrix products, arithmetic and copies ran while one was open for 3% -> 6% of each run, Pallas kernels for 14% -> 16%
where the time goes in v1:
time: 257 us
  starting transfers between devices  100 us (39%)
  waiting for transfers between devices  96.7 us (38%)
  Pallas kernels  40.9 us (16%)
  local copies, waits for them, and re-layouts  13.9 us (5%)
  other arithmetic  4.75 us (2%)
    pallas_call x9, Pallas kernels, products(): pl.pallas_call(product_kernel, grid_spec=pltpu.PrefetchScalarGridSpec(num...  40.9 us
    ppermute x9, starting transfers between devices, chain(): two = lax.ppermute(sent, ('y', 'c'), flips(True))  38.7 us
    ppermute x22, starting transfers between devices, swap(): return lax.ppermute(x, axis, [(0, 1), (1, 0)])  34.7 us
    ppermute x9, waiting for transfers between devices, chain(): two = lax.ppermute(sent, ('y', 'c'), flips(True))  28 us
    ppermute x22, waiting for transfers between devices, swap(): return lax.ppermute(x, axis, [(0, 1), (1, 0)])  24.8 us
    ppermute x9, waiting for transfers between devices, chain(): side = lax.ppermute(pair, ('z', 'c'), flips(True))  22.5 us
    ppermute x9, starting transfers between devices, chain(): side = lax.ppermute(pair, ('z', 'c'), flips(True))  15.5 us
    ppermute x9, waiting for transfers between devices, chain(): rest = lax.ppermute(four, ('z', 'c'), flips(False))  14.2 us
  transfers between devices with their start and end apart: 58, of which 32 were waited for; matrix products, arithmetic and copies ran while one was open for 6% of the time, Pallas kernels for 16%

profile of v1, /device:TPU:1, one launch (start us, length us, event | category | flops | bytes accessed | tf_op | source)
XLA Modules:
  0.0 257.1 jit_solution(16790754504594732413)
XLA Ops:
  2.7 4.8 %copy.19 = bf16[64,1,2,128,128]{4,3,0,2,1:T(8,128)(2,1)} copy(bf16[64,1,2,128,128]{4,3,2,1,0:T(8,128)(2,1)} %param.7) | data formatting | bytes 8388608 | tf_op args[1]
  9.9 4.8 %collective-permute-done.3 = bf16[768,128]{1,0:T(8,128)(2,1)S(1)} collective-permute-done((bf16[768,128]{1,0:T(8,128)(2,1)S(1)}, bf16[768,128]{1,0:T(8,128)(2,1)S(1)}, u32[]{:S(2)}, u32[]{:S(2)}) %collective-permute-start.3) | collective-permute-done | bytes 196640 | tf_op jit(solution)/shard_map/ppermute | solution.py:23
  19.0 4.8 %collective-permute-done.4 = bf16[1536,128]{1,0:T(8,128)(2,1)S(1)} collective-permute-done((bf16[1536,128]{1,0:T(8,128)(2,1)S(1)}, bf16[1536,128]{1,0:T(8,128)(2,1)S(1)}, u32[]{:S(2)}, u32[]{:S(2)}) %collective-permute-start.4) | collective-permute-done | bytes 393248 | tf_op jit(solution)/shard_map/ppermute | solution.py:116
  35.4 6.7 %collective-permute-done.5.refs_1_ = bf16[3072,128]{1,0:T(8,128)(2,1)S(1)} collective-permute-done((bf16[3072,128]{1,0:T(8,128)(2,1)S(1)}, bf16[3072,128]{1,0:T(8,128)(2,1)S(1)}, u32[]{:S(2)}, u32[]{:S(2)}) %collective-permute-start.5) | collective-permute-done | bytes 786464 | tf_op jit(solution)/shard_map/ppermute | solution.py:118
  42.1 4.5 %products.9 = bf16[6144,128]{1,0:T(8,128)(2,1)S(1)} custom-call(s32[16]{0:T(128)S(1)} %add.227.order, s32[256]{0:T(256)S(1)} %reshape.32.picks, bf16[64,128,512]{2,1,0:T(8,128)(2,1)S(1)} %pad_maximum_fusion.merged, bf16[3072,128]{1,0:T(8,128)(2,1)S(1)} %pad_maximum_fusion.1.refs_0_, bf16[3072,128]{1,0:T(8,128)(2,1)S(1)} %collective-permute-done.5.refs_1_), custom_call_target="tpu_custom_call" | custom-call | flops 805306368 | bytes 4194304 | tf_op jit(solution)/shard_map/products/pallas_call | solution.py:54
  51.5 4.6 %collective-permute-done.9 = bf16[1280,128]{1,0:T(8,128)(2,1)S(1)} collective-permute-done((bf16[1280,128]{1,0:T(8,128)(2,1)S(1)}, bf16[1280,128]{1,0:T(8,128)(2,1)S(1)}, u32[]{:S(2)}, u32[]{:S(2)}) %collective-permute-start.9) | collective-permute-done | bytes 327712 | tf_op jit(solution)/shard_map/ppermute | solution.py:116
  64.8 4.6 %products.10 = bf16[5120,128]{1,0:T(8,128)(2,1)S(1)} custom-call(s32[16]{0:T(128)S(1)} %add.227.order, s32[256]{0:T(256)S(1)} %reshape.32.picks, bf16[64,128,512]{2,1,0:T(8,128)(2,1)S(1)} %pad_maximum_fusion.merged, bf16[2560,128]{1,0:T(8,128)(2,1)S(1)} %pad_maximum_fusion.5.refs_0_, bf16[2560,128]{1,0:T(8,128)(2,1)S(1)} %collective-permute-done.12.refs_1_), custom_call_target="tpu_custom_call" | custom-call | flops 671088640 | bytes 4194304 | tf_op jit(solution)/shard_map/products/pallas_call | solution.py:54
  72.3 4.6 %products.11 = bf16[5120,128]{1,0:T(8,128)(2,1)S(1)} custom-call(s32[16]{0:T(128)S(1)} %add.227.order, s32[256]{0:T(256)S(1)} %reshape.32.picks, bf16[64,128,512]{2,1,0:T(8,128)(2,1)S(1)} %pad_maximum_fusion.merged, bf16[2560,128]{1,0:T(8,128)(2,1)S(1)} %pad_maximum_fusion.4.refs_0_, bf16[2560,128]{1,0:T(8,128)(2,1)S(1)} %collective-permute-done.14.refs_1_), custom_call_target="tpu_custom_call" | custom-call | flops 671088640 | bytes 4194304 | tf_op jit(solution)/shard_map/products/pallas_call | solution.py:54
  108.3 4.5 %products.12 = bf16[6144,128]{1,0:T(8,128)(2,1)S(1)} custom-call(s32[16]{0:T(128)S(1)} %add.227.order, s32[256]{0:T(256)S(1)} %reshape.32.picks, bf16[64,128,512]{2,1,0:T(8,128)(2,1)S(1)} %pad_maximum_fusion.merged, bf16[3072,128]{1,0:T(8,128)(2,1)S(1)} %pad_maximum_fusion.2.refs_0_, bf16[3072,128]{1,0:T(8,128)(2,1)S(1)} %collective-permute-done.20.refs_1_), custom_call_target="tpu_custom_call" | custom-call | flops 805306368 | bytes 4194304 | tf_op jit(solution)/shard_map/products/pallas_call | solution.py:54
  127.6 4.6 %products.13 = bf16[5120,128]{1,0:T(8,128)(2,1)S(1)} custom-call(s32[16]{0:T(128)S(1)} %add.227.order, s32[256]{0:T(256)S(1)} %reshape.32.picks, bf16[64,128,512]{2,1,0:T(8,128)(2,1)S(1)} %pad_maximum_fusion.merged, bf16[2560,128]{1,0:T(8,128)(2,1)S(1)} %pad_maximum_fusion.7.refs_0_, bf16[2560,128]{1,0:T(8,128)(2,1)S(1)} %collective-permute-done.30.refs_1_), custom_call_target="tpu_custom_call" | custom-call | flops 671088640 | bytes 4194304 | tf_op jit(solution)/shard_map/products/pallas_call | solution.py:54
  132.4 4.0 %collective-permute-done.29 = bf16[1536,128]{1,0:T(8,128)(2,1)S(1)} collective-permute-done((bf16[1536,128]{1,0:T(8,128)(2,1)S(1)}, bf16[1536,128]{1,0:T(8,128)(2,1)S(1)}, u32[]{:S(2)}, u32[]{:S(2)}) %collective-permute-start.29) | collective-permute-done | bytes 393248 | tf_op jit(solution)/shard_map/ppermute | solution.py:122
  138.3 4.6 %products.14 = bf16[5120,128]{1,0:T(8,128)(2,1)S(1)} custom-call(s32[16]{0:T(128)S(1)} %add.227.order, s32[256]{0:T(256)S(1)} %reshape.32.picks, bf16[64,128,512]{2,1,0:T(8,128)(2,1)S(1)} %pad_maximum_fusion.merged, bf16[2560,128]{1,0:T(8,128)(2,1)S(1)} %pad_maximum_fusion.6.refs_0_, bf16[2560,128]{1,0:T(8,128)(2,1)S(1)} %collective-permute-done.32.refs_1_), custom_call_target="tpu_custom_call" | custom-call | flops 671088640 | bytes 4194304 | tf_op jit(solution)/shard_map/products/pallas_call | solution.py:54
  150.7 5.7 %collective-permute-done.36 = bf16[1280,128]{1,0:T(8,128)(2,1)S(1)} collective-permute-done((bf16[1280,128]{1,0:T(8,128)(2,1)S(1)}, bf16[1280,128]{1,0:T(8,128)(2,1)S(1)}, u32[]{:S(2)}, u32[]{:S(2)}) %collective-permute-start.36) | collective-permute-done | bytes 327712 | tf_op jit(solution)/shard_map/ppermute | solution.py:122
  161.0 6.0 %collective-permute-done.40 = bf16[1280,128]{1,0:T(8,128)(2,1)S(1)} collective-permute-done((bf16[1280,128]{1,0:T(8,128)(2,1)S(1)}, bf16[1280,128]{1,0:T(8,128)(2,1)S(1)}, u32[]{:S(2)}, u32[]{:S(2)}) %collective-permute-start.40) | collective-permute-done | bytes 327712 | tf_op jit(solution)/shard_map/ppermute | solution.py:122
  167.5 5.3 %collective-permute-done.42 = bf16[640,128]{1,0:T(8,128)(2,1)S(1)} collective-permute-done((bf16[640,128]{1,0:T(8,128)(2,1)S(1)}, bf16[640,128]{1,0:T(8,128)(2,1)S(1)}, u32[]{:S(2)}, u32[]{:S(2)}) %collective-permute-start.42) | collective-permute-done | bytes 163872 | tf_op jit(solution)/shard_map/ppermute | solution.py:23
  173.1 4.5 %products.15 = bf16[6144,128]{1,0:T(8,128)(2,1)S(1)} custom-call(s32[16]{0:T(128)S(1)} %add.227.order, s32[256]{0:T(256)S(1)} %reshape.32.picks, bf16[64,128,512]{2,1,0:T(8,128)(2,1)S(1)} %pad_maximum_fusion.merged, bf16[3072,128]{1,0:T(8,128)(2,1)S(1)} %pad_maximum_fusion.3.refs_0_, bf16[3072,128]{1,0:T(8,128)(2,1)S(1)} %collective-permute-done.38.refs_1_), custom_call_target="tpu_custom_call" | custom-call | flops 805306368 | bytes 4194304 | tf_op jit(solution)/shard_map/products/pallas_call | solution.py:54
  183.1 7.1 %collective-permute-done.45 = bf16[1280,128]{1,0:T(8,128)(2,1)S(1)} collective-permute-done((bf16[1280,128]{1,0:T(8,128)(2,1)S(1)}, bf16[1280,128]{1,0:T(8,128)(2,1)S(1)}, u32[]{:S(2)}, u32[]{:S(2)}) %collective-permute-start.45) | collective-permute-done | bytes 327712 | tf_op jit(solution)/shard_map/ppermute | solution.py:116
  190.5 4.5 %collective-permute-start.47 = (bf16[1536,128]{1,0:T(8,128)(2,1)S(1)}, bf16[1536,128]{1,0:T(8,128)(2,1)S(1)}, u32[]{:S(2)}, u32[]{:S(2)}) collective-permute-start(bf16[1536,128]{1,0:T(8,128)(2,1)S(1)} %add_convert_fusion), channel_id=1, source_target_pairs={{0,4},{1,13},{4,0},{5,9},{8,12},{9,5},{12,8},{13,1},{2,6},{3,15},{... | collective-permute-start | bytes 1179656 | tf_op jit(solution)/shard_map/ppermute | solution.py:122
  195.0 4.6 %products.16 = bf16[5120,128]{1,0:T(8,128)(2,1)S(1)} custom-call(s32[16]{0:T(128)S(1)} %add.227.order, s32[256]{0:T(256)S(1)} %reshape.32.picks, bf16[64,128,512]{2,1,0:T(8,128)(2,1)S(1)} %pad_maximum_fusion.merged, bf16[2560,128]{1,0:T(8,128)(2,1)S(1)} %pad_maximum_fusion.9.refs_0_, bf16[2560,128]{1,0:T(8,128)(2,1)S(1)} %collective-permute-done.48.refs_1_), custom_call_target="tpu_custom_call" | custom-call | flops 671088640 | bytes 4194304 | tf_op jit(solution)/shard_map/products/pallas_call | solution.py:54
  201.6 4.6 %products.17 = bf16[5120,128]{1,0:T(8,128)(2,1)S(1)} custom-call(s32[16]{0:T(128)S(1)} %add.227.order, s32[256]{0:T(256)S(1)} %reshape.32.picks, bf16[64,128,512]{2,1,0:T(8,128)(2,1)S(1)} %pad_maximum_fusion.merged, bf16[2560,128]{1,0:T(8,128)(2,1)S(1)} %pad_maximum_fusion.8.refs_0_, bf16[2560,128]{1,0:T(8,128)(2,1)S(1)} %collective-permute-done.51.refs_1_), custom_call_target="tpu_custom_call" | custom-call | flops 671088640 | bytes 4194304 | tf_op jit(solution)/shard_map/products/pallas_call | solution.py:54
  209.5 7.9 %collective-permute-start.52 = (bf16[1280,128]{1,0:T(8,128)(2,1)S(1)}, bf16[1280,128]{1,0:T(8,128)(2,1)S(1)}, u32[]{:S(2)}, u32[]{:S(2)}) collective-permute-start(bf16[1280,128]{1,0:T(8,128)(2,1)S(1)} %add_convert_fusion.4), channel_id=1, source_target_pairs={{0,4},{1,13},{4,0},{5,9},{8,12},{9,5},{12,8},{13,1},{2,6},{3,15},{... | collective-permute-start | bytes 983048 | tf_op jit(solution)/shard_map/ppermute | solution.py:122
  218.9 8.9 %collective-permute-start.55 = (bf16[1280,128]{1,0:T(8,128)(2,1)S(1)}, bf16[1280,128]{1,0:T(8,128)(2,1)S(1)}, u32[]{:S(2)}, u32[]{:S(2)}) collective-permute-start(bf16[1280,128]{1,0:T(8,128)(2,1)S(1)} %add_convert_fusion.3), channel_id=1, source_target_pairs={{0,4},{1,13},{4,0},{5,9},{8,12},{9,5},{12,8},{13,1},{2,6},{3,15},{... | collective-permute-start | bytes 983048 | tf_op jit(solution)/shard_map/ppermute | solution.py:122
  230.0 6.2 %collective-permute-done.55 = bf16[1280,128]{1,0:T(8,128)(2,1)S(1)} collective-permute-done((bf16[1280,128]{1,0:T(8,128)(2,1)S(1)}, bf16[1280,128]{1,0:T(8,128)(2,1)S(1)}, u32[]{:S(2)}, u32[]{:S(2)}) %collective-permute-start.55) | collective-permute-done | bytes 327712 | tf_op jit(solution)/shard_map/ppermute | solution.py:122
  242.2 12.5 %collective-permute-start.57 = (bf16[4,256,128]{2,1,0:T(8,128)(2,1)S(1)}, bf16[4,256,128]{2,1,0:T(8,128)(2,1)S(1)}, u32[]{:S(2)}, u32[]{:S(2)}) collective-permute-start(bf16[4,256,128]{2,1,0:T(8,128)(2,1)S(1)} %get-tuple-element.124), channel_id=1, source_target_pairs={{0,1},{1,0},{2,3},{3,2},{4,5},{5,4},{6,7},{7,6},{8,9},{9,8},{10,11... | collective-permute-start | bytes 786440 | tf_op jit(solution)/shard_map/ppermute | solution.py:23
  (187 shorter events, 121.7 us)
Async XLA Ops:
  7.8 23.6 %collective-permute-start.2 = (bf16[64,2,128,128]{3,2,0,1:T(8,128)(2,1)}, bf16[64,2,128,128]{3,2,0,1:T(8,128)(2,1)}, u32[]{:S(2)}, u32[]{:S(2)}) collective-permute-start(bf16[64,2,128,128]{3,2,0,1:T(8,128)(2,1)} %bitcast.56), channel_id=1, source_target_pairs={{0,1},{1,0},{2,3},{3,2},{4,5},{5,4},{6,7},{7,6},{8,9},{9,8},{10,11... | collective-permute-start | bytes 12582920 | tf_op jit(solution)/shard_map/ppermute | solution.py:23
  28.0 14.1 %collective-permute-start.5 = (bf16[3072,128]{1,0:T(8,128)(2,1)S(1)}, bf16[3072,128]{1,0:T(8,128)(2,1)S(1)}, u32[]{:S(2)}, u32[]{:S(2)}) collective-permute-start(bf16[3072,128]{1,0:T(8,128)(2,1)S(1)} %pad_maximum_fusion.1.refs_0_), channel_id=1, source_target_pairs={{0,48},{1,17},{16,32},{17,1},{32,16},{33,49},{48,0},{49,33},{2,50}... | collective-permute-start | bytes 2359304 | tf_op jit(solution)/shard_map/ppermute | solution.py:118
  28.1 20.0 %collective-permute-start.8 = (bf16[640,128]{1,0:T(8,128)(2,1)S(1)}, bf16[640,128]{1,0:T(8,128)(2,1)S(1)}, u32[]{:S(2)}, u32[]{:S(2)}) collective-permute-start(bf16[640,128]{1,0:T(8,128)(2,1)S(1)} %bitcast.63), channel_id=1, source_target_pairs={{0,64},{64,0},{1,65},{65,1},{2,66},{66,2},{3,67},{67,3},{4,68},{68... | collective-permute-start | bytes 491528 | tf_op jit(solution)/shard_map/ppermute | solution.py:23
  29.9 21.5 %collective-permute-start.10 = (bf16[1280,128]{1,0:T(8,128)(2,1)S(1)}, bf16[1280,128]{1,0:T(8,128)(2,1)S(1)}, u32[]{:S(2)}, u32[]{:S(2)}) collective-permute-start(bf16[1280,128]{1,0:T(8,128)(2,1)S(1)} %pad_maximum_fusion.14), channel_id=1, source_target_pairs={{0,16},{1,49},{16,0},{17,33},{32,48},{33,17},{48,32},{49,1},{2,18}... | collective-permute-start | bytes 983048 | tf_op jit(solution)/shard_map/ppermute | solution.py:116
  46.6 11.2 %collective-permute-start.7 = (bf16[3072,128]{1,0:T(8,128)(2,1)S(1)}, bf16[3072,128]{1,0:T(8,128)(2,1)S(1)}, u32[]{:S(2)}, u32[]{:S(2)}) collective-permute-start(bf16[3072,128]{1,0:T(8,128)(2,1)S(1)} %slice.278), channel_id=1, source_target_pairs={{0,12},{1,5},{4,8},{5,1},{8,4},{9,13},{12,0},{13,9},{2,14},{3,7},{... | collective-permute-start | bytes 2359304 | tf_op jit(solution)/shard_map/ppermute | solution.py:120
  51.4 13.3 %collective-permute-start.12 = (bf16[2560,128]{1,0:T(8,128)(2,1)S(1)}, bf16[2560,128]{1,0:T(8,128)(2,1)S(1)}, u32[]{:S(2)}, u32[]{:S(2)}) collective-permute-start(bf16[2560,128]{1,0:T(8,128)(2,1)S(1)} %pad_maximum_fusion.5.refs_0_), channel_id=1, source_target_pairs={{0,48},{1,17},{16,32},{17,1},{32,16},{33,49},{48,0},{49,33},{2,50}... | collective-permute-start | bytes 1966088 | tf_op jit(solution)/shard_map/ppermute | solution.py:118
  58.0 11.7 %collective-permute-start.11 = (bf16[1536,128]{1,0:T(8,128)(2,1)S(1)}, bf16[1536,128]{1,0:T(8,128)(2,1)S(1)}, u32[]{:S(2)}, u32[]{:S(2)}) collective-permute-start(bf16[1536,128]{1,0:T(8,128)(2,1)S(1)} %add_convert_fusion.2), channel_id=1, source_target_pairs={{0,4},{1,13},{4,0},{5,9},{8,12},{9,5},{12,8},{13,1},{2,6},{3,15},{... | collective-permute-start | bytes 1179656 | tf_op jit(solution)/shard_map/ppermute | solution.py:122
  60.8 11.5 %collective-permute-start.14 = (bf16[2560,128]{1,0:T(8,128)(2,1)S(1)}, bf16[2560,128]{1,0:T(8,128)(2,1)S(1)}, u32[]{:S(2)}, u32[]{:S(2)}) collective-permute-start(bf16[2560,128]{1,0:T(8,128)(2,1)S(1)} %pad_maximum_fusion.4.refs_0_), channel_id=1, source_target_pairs={{0,48},{1,17},{16,32},{17,1},{32,16},{33,49},{48,0},{49,33},{2,50}... | collective-permute-start | bytes 1966088 | tf_op jit(solution)/shard_map/ppermute | solution.py:118
  93.9 14.4 %collective-permute-start.20 = (bf16[3072,128]{1,0:T(8,128)(2,1)S(1)}, bf16[3072,128]{1,0:T(8,128)(2,1)S(1)}, u32[]{:S(2)}, u32[]{:S(2)}) collective-permute-start(bf16[3072,128]{1,0:T(8,128)(2,1)S(1)} %pad_maximum_fusion.2.refs_0_), channel_id=1, source_target_pairs={{0,48},{1,17},{16,32},{17,1},{32,16},{33,49},{48,0},{49,33},{2,50}... | collective-permute-start | bytes 2359304 | tf_op jit(solution)/shard_map/ppermute | solution.py:118
  123.9 12.5 %collective-permute-start.29 = (bf16[1536,128]{1,0:T(8,128)(2,1)S(1)}, bf16[1536,128]{1,0:T(8,128)(2,1)S(1)}, u32[]{:S(2)}, u32[]{:S(2)}) collective-permute-start(bf16[1536,128]{1,0:T(8,128)(2,1)S(1)} %add_convert_fusion.1), channel_id=1, source_target_pairs={{0,4},{1,13},{4,0},{5,9},{8,12},{9,5},{12,8},{13,1},{2,6},{3,15},{... | collective-permute-start | bytes 1179656 | tf_op jit(solution)/shard_map/ppermute | solution.py:122
  126.6 11.8 %collective-permute-start.32 = (bf16[2560,128]{1,0:T(8,128)(2,1)S(1)}, bf16[2560,128]{1,0:T(8,128)(2,1)S(1)}, u32[]{:S(2)}, u32[]{:S(2)}) collective-permute-start(bf16[2560,128]{1,0:T(8,128)(2,1)S(1)} %pad_maximum_fusion.6.refs_0_), channel_id=1, source_target_pairs={{0,48},{1,17},{16,32},{17,1},{32,16},{33,49},{48,0},{49,33},{2,50}... | collective-permute-start | bytes 1966088 | tf_op jit(solution)/shard_map/ppermute | solution.py:118
  132.2 13.7 %collective-permute-start.34 = (bf16[2560,128]{1,0:T(8,128)(2,1)S(1)}, bf16[2560,128]{1,0:T(8,128)(2,1)S(1)}, u32[]{:S(2)}, u32[]{:S(2)}) collective-permute-start(bf16[2560,128]{1,0:T(8,128)(2,1)S(1)} %slice.314), channel_id=1, source_target_pairs={{0,12},{1,5},{4,8},{5,1},{8,4},{9,13},{12,0},{13,9},{2,14},{3,7},{... | collective-permute-start | bytes 1966088 | tf_op jit(solution)/shard_map/ppermute | solution.py:120
  143.0 13.6 %collective-permute-start.37 = (bf16[2560,128]{1,0:T(8,128)(2,1)S(1)}, bf16[2560,128]{1,0:T(8,128)(2,1)S(1)}, u32[]{:S(2)}, u32[]{:S(2)}) collective-permute-start(bf16[2560,128]{1,0:T(8,128)(2,1)S(1)} %slice.320), channel_id=1, source_target_pairs={{0,12},{1,5},{4,8},{5,1},{8,4},{9,13},{12,0},{13,9},{2,14},{3,7},{... | collective-permute-start | bytes 1966088 | tf_op jit(solution)/shard_map/ppermute | solution.py:120
  160.4 12.8 %collective-permute-start.38 = (bf16[3072,128]{1,0:T(8,128)(2,1)S(1)}, bf16[3072,128]{1,0:T(8,128)(2,1)S(1)}, u32[]{:S(2)}, u32[]{:S(2)}) collective-permute-start(bf16[3072,128]{1,0:T(8,128)(2,1)S(1)} %pad_maximum_fusion.3.refs_0_), channel_id=1, source_target_pairs={{0,48},{1,17},{16,32},{17,1},{32,16},{33,49},{48,0},{49,33},{2,50}... | collective-permute-start | bytes 2359304 | tf_op jit(solution)/shard_map/ppermute | solution.py:118
  177.7 12.7 %collective-permute-start.43 = (bf16[3072,128]{1,0:T(8,128)(2,1)S(1)}, bf16[3072,128]{1,0:T(8,128)(2,1)S(1)}, u32[]{:S(2)}, u32[]{:S(2)}) collective-permute-start(bf16[3072,128]{1,0:T(8,128)(2,1)S(1)} %slice.332), channel_id=1, source_target_pairs={{0,12},{1,5},{4,8},{5,1},{8,4},{9,13},{12,0},{13,9},{2,14},{3,7},{... | collective-permute-start | bytes 2359304 | tf_op jit(solution)/shard_map/ppermute | solution.py:120
  179.1 11.1 %collective-permute-start.45 = (bf16[1280,128]{1,0:T(8,128)(2,1)S(1)}, bf16[1280,128]{1,0:T(8,128)(2,1)S(1)}, u32[]{:S(2)}, u32[]{:S(2)}) collective-permute-start(bf16[1280,128]{1,0:T(8,128)(2,1)S(1)} %pad_maximum_fusion.19), channel_id=1, source_target_pairs={{0,16},{1,49},{16,0},{17,33},{32,48},{33,17},{48,32},{49,1},{2,18}... | collective-permute-start | bytes 983048 | tf_op jit(solution)/shard_map/ppermute | solution.py:116
  180.6 14.4 %collective-permute-start.48 = (bf16[2560,128]{1,0:T(8,128)(2,1)S(1)}, bf16[2560,128]{1,0:T(8,128)(2,1)S(1)}, u32[]{:S(2)}, u32[]{:S(2)}) collective-permute-start(bf16[2560,128]{1,0:T(8,128)(2,1)S(1)} %pad_maximum_fusion.9.refs_0_), channel_id=1, source_target_pairs={{0,48},{1,17},{16,32},{17,1},{32,16},{33,49},{48,0},{49,33},{2,50}... | collective-permute-start | bytes 1966088 | tf_op jit(solution)/shard_map/ppermute | solution.py:118
  190.2 11.4 %collective-permute-start.51 = (bf16[2560,128]{1,0:T(8,128)(2,1)S(1)}, bf16[2560,128]{1,0:T(8,128)(2,1)S(1)}, u32[]{:S(2)}, u32[]{:S(2)}) collective-permute-start(bf16[2560,128]{1,0:T(8,128)(2,1)S(1)} %pad_maximum_fusion.8.refs_0_), channel_id=1, source_target_pairs={{0,48},{1,17},{16,32},{17,1},{32,16},{33,49},{48,0},{49,33},{2,50}... | collective-permute-start | bytes 1966088 | tf_op jit(solution)/shard_map/ppermute | solution.py:118
  190.5 15.8 %collective-permute-start.47 = (bf16[1536,128]{1,0:T(8,128)(2,1)S(1)}, bf16[1536,128]{1,0:T(8,128)(2,1)S(1)}, u32[]{:S(2)}, u32[]{:S(2)}) collective-permute-start(bf16[1536,128]{1,0:T(8,128)(2,1)S(1)} %add_convert_fusion), channel_id=1, source_target_pairs={{0,4},{1,13},{4,0},{5,9},{8,12},{9,5},{12,8},{13,1},{2,6},{3,15},{... | collective-permute-start | bytes 1179656 | tf_op jit(solution)/shard_map/ppermute | solution.py:122
  206.4 12.4 %collective-permute-start.53 = (bf16[2560,128]{1,0:T(8,128)(2,1)S(1)}, bf16[2560,128]{1,0:T(8,128)(2,1)S(1)}, u32[]{:S(2)}, u32[]{:S(2)}) collective-permute-start(bf16[2560,128]{1,0:T(8,128)(2,1)S(1)} %slice.350), channel_id=1, source_target_pairs={{0,12},{1,5},{4,8},{5,1},{8,4},{9,13},{12,0},{13,9},{2,14},{3,7},{... | collective-permute-start | bytes 1966088 | tf_op jit(solution)/shard_map/ppermute | solution.py:120
  207.8 20.1 %collective-permute-start.49 = (bf16[768,128]{1,0:T(8,128)(2,1)S(1)}, bf16[768,128]{1,0:T(8,128)(2,1)S(1)}, u32[]{:S(2)}, u32[]{:S(2)}) collective-permute-start(bf16[768,128]{1,0:T(8,128)(2,1)S(1)} %add_convert_fusion.9), channel_id=1, source_target_pairs={{0,2},{2,0},{1,3},{3,1},{4,6},{6,4},{5,7},{7,5},{8,10},{10,8},{9,1... | collective-permute-start | bytes 589832 | tf_op jit(solution)/shard_map/ppermute | solution.py:23
  209.5 18.5 %collective-permute-start.52 = (bf16[1280,128]{1,0:T(8,128)(2,1)S(1)}, bf16[1280,128]{1,0:T(8,128)(2,1)S(1)}, u32[]{:S(2)}, u32[]{:S(2)}) collective-permute-start(bf16[1280,128]{1,0:T(8,128)(2,1)S(1)} %add_convert_fusion.4), channel_id=1, source_target_pairs={{0,4},{1,13},{4,0},{5,9},{8,12},{9,5},{12,8},{13,1},{2,6},{3,15},{... | collective-permute-start | bytes 983048 | tf_op jit(solution)/shard_map/ppermute | solution.py:122
  218.9 17.3 %collective-permute-start.55 = (bf16[1280,128]{1,0:T(8,128)(2,1)S(1)}, bf16[1280,128]{1,0:T(8,128)(2,1)S(1)}, u32[]{:S(2)}, u32[]{:S(2)}) collective-permute-start(bf16[1280,128]{1,0:T(8,128)(2,1)S(1)} %add_convert_fusion.3), channel_id=1, source_target_pairs={{0,4},{1,13},{4,0},{5,9},{8,12},{9,5},{12,8},{13,1},{2,6},{3,15},{... | collective-permute-start | bytes 983048 | tf_op jit(solution)/shard_map/ppermute | solution.py:122
  242.2 13.7 %collective-permute-start.57 = (bf16[4,256,128]{2,1,0:T(8,128)(2,1)S(1)}, bf16[4,256,128]{2,1,0:T(8,128)(2,1)S(1)}, u32[]{:S(2)}, u32[]{:S(2)}) collective-permute-start(bf16[4,256,128]{2,1,0:T(8,128)(2,1)S(1)} %get-tuple-element.124), channel_id=1, source_target_pairs={{0,1},{1,0},{2,3},{3,2},{4,5},{5,4},{6,7},{7,6},{8,9},{9,8},{10,11... | collective-permute-start | bytes 786440 | tf_op jit(solution)/shard_map/ppermute | solution.py:23
  (38 other events, 297.5 us)

commit v2 on v1

--- a/solution.py
+++ b/solution.py
@@ -10,8 +10,8 @@
 
 DEGREE = 3
 BLK = 128
-CHUNKS = (96, 80, 80)
-TURNS = (0, 0, 0, 1, 2, 1, 0, 2, 1, 2, 0, 1, 0, 2, 0, 1, 0, 2, 1, 0, 2, 1, 2, 1, 0, 2, 1, 2, 0, 1, 0, 2, 0, 1, 0, 2, 1, 0, 2, 1, 2, 1, 0, 2, 1, 2, 0, 1, 0, 2, 1, 2, 1, 2)
+CHUNKS = (64, 64, 64, 64)
+TURNS = (0, 1, 0, 1, 0, 2, 3, 1, 2, 0, 3, 2, 1, 3, 0, 2, 0, 1, 3, 0, 1, 2, 0, 1, 3, 2, 1, 0, 3, 2, 1, 3, 0, 2, 1, 3, 2, 0, 3, 1, 2, 0, 3, 1, 0, 2, 1, 0, 3, 2, 1, 0, 3, 2, 1, 3, 2, 0, 3, 2, 1, 3, 0, 2, 1, 3, 1, 0, 2, 3, 2, 3)
 UNIT = 8
 
 
@@ -23,7 +23,7 @@
     return lax.ppermute(x, axis, [(0, 1), (1, 0)])
 
 
-def product_kernel(order, picks, merged, *refs):
+def product_kernel(order, picks, own, other, *refs):
     *pieces, out, held = refs
     step = pl.program_id(0)
     size = held.shape[0] // (8 * UNIT + 1)
@@ -43,12 +43,13 @@
             picked = jnp.concatenate(
                 [held[pl.ds(pl.multiple_of(picks[a * 4 + k] * size, 16), size), :] for k in range(4)], axis=1
             )
-            total = lax.dot_general(picked, merged[a], (((1,), (1,)), ((), ())), preferred_element_type=jnp.float32)
+            row = jnp.concatenate([own[a, 0], own[a, 1], other[a, 0], other[a, 1]], axis=1)
+            total = lax.dot_general(picked, row, (((1,), (1,)), ((), ())), preferred_element_type=jnp.float32)
             at = pl.multiple_of((step * UNIT + half * 4 + j) * size, 16)
             out[pl.ds(at, size), :] = total.astype(out.dtype)
 
 
-def products(order, picks, merged, pieces):
+def products(order, picks, own, other, pieces):
     rows = sum(piece.shape[0] for piece in pieces)
     whole = pl.BlockSpec(memory_space=pltpu.VMEM)
     return pl.pallas_call(
@@ -56,7 +57,7 @@
         grid_spec=pltpu.PrefetchScalarGridSpec(
             num_scalar_prefetch=2,
             grid=(8,),
-            in_specs=[whole] * (1 + len(pieces)),
+            in_specs=[whole] * (2 + len(pieces)),
             out_specs=whole,
             scratch_shapes=[pltpu.VMEM((rows + rows // (8 * UNIT), BLK), jnp.bfloat16)],
         ),
@@ -64,7 +65,7 @@
         compiler_params=pltpu.CompilerParams(vmem_limit_bytes=24 << 20),
         cost_estimate=pl.CostEstimate(flops=2 * rows * 512 * 128, bytes_accessed=4 << 20, transcendentals=0),
         name="products",
-    )(order, picks, merged, *pieces)
+    )(order, picks, own, other, *pieces)
 
 
 def add(*terms):
@@ -89,7 +90,6 @@
     own = tiles[:, 0]
     own, first = lax.optimization_barrier((own, first))
     other = swap(own, "c")
-    merged = jnp.concatenate([own[:, 0], own[:, 1], other[:, 0], other[:, 1]], axis=2)
 
     r, i = tile_col[:, 0] // 4, tile_col[:, 0] % 4
     dx, dz = (r // 4) ^ xl, (r & 3) ^ z
@@ -99,7 +99,11 @@
         slot = jnp.where(dz == 0, 0, jnp.where(dz == 2, 3, jnp.where(dz == 1 + 2 * core, 1, 2)))
         return jnp.where(live, (slot * 2 + dx) * UNIT + shift + i, 8 * UNIT)
 
-    picks = jnp.concatenate([code(c, 0), swap(code(1 - c, 4), "c")], axis=1).reshape(-1)
+    codes = code(c, 0), swap(code(1 - c, 4), "c")
+    picks = jnp.concatenate(codes, axis=1).reshape(-1)
+    own, other = (
+        jnp.where((at < 8 * UNIT)[:, :, None, None], t, jnp.zeros((), t.dtype)) for at, t in zip(codes, (own, other))
+    )
 
     far, near = 3 - 2 * c, 1 + 2 * c
     dy = jnp.stack([far, far, jnp.int32(2), jnp.int32(2), near, near, jnp.int32(0), jnp.int32(0)])
@@ -116,7 +120,7 @@
             side = lax.ppermute(pair, ("z", "c"), flips(True))
             four = yield jnp.concatenate([pair, side], axis=0)
             rest = lax.ppermute(four, ("z", "c"), flips(False))
-            p = yield products(order, picks, merged, (four, rest))
+            p = yield products(order, picks, own, other, (four, rest))
             one = lax.ppermute(p[: 4 * u], ("y", "c"), flips(False))
             sent = yield add(p[4 * u : 6 * u], one[2 * u :]).astype(p.dtype)
             two = lax.ppermute(sent, ("y", "c"), flips(True))

time: 257 us -> 236 us (0.918)
  waiting for transfers between devices: 96.7 us -> 55.8 us
  Pallas kernels: 40.9 us -> 54.6 us
  local copies, waits for them, and re-layouts: 13.9 us -> 3.47 us
  starting transfers between devices: 100 us -> 110 us
  other arithmetic: 4.75 us -> 11.4 us
    ppermute x9 -> x12, waiting for transfers between devices: 22.5 us -> 4.56 us  [chain(): side = lax.ppermute(pair, ('z', 'c'), flips(True))]
    ppermute x9 -> x12, waiting for transfers between devices: 28 us -> 13.7 us  [chain(): two = lax.ppermute(sent, ('y', 'c'), flips(True))]
    pallas_call x9 -> x12, Pallas kernels: 40.9 us -> 54.6 us  [products(): pl.pallas_call(product_kernel, grid_spec=pltpu.PrefetchScalarGridSpec(num...]
    ppermute x9 -> x12, starting transfers between devices: 15.5 us -> 24.1 us  [chain(): side = lax.ppermute(pair, ('z', 'c'), flips(True))]
    ppermute x9 -> x12, waiting for transfers between devices: 14.2 us -> 6.72 us  [chain(): rest = lax.ppermute(four, ('z', 'c'), flips(False))]
    squeeze x2 -> x0, local copies, waits for them, and re-layouts: 5.59 us -> none  [the longest x1 2.8 us: body(): other[:, 0]]
    ppermute x9 -> x12, starting transfers between devices: 38.7 us -> 33.2 us  [chain(): two = lax.ppermute(sent, ('y', 'c'), flips(True))]
    unnamed x11 -> x2, local copies, waits for them, and re-layouts: 5.42 us -> 0.34 us
  transfers between devices with their start and end apart: 58 -> 76, of which waited for: 32 -> 36; matrix products, arithmetic and copies ran while one was open for 6% -> 5% of each run, Pallas kernels for 16% -> 23%
where the time goes in v2:
time: 236 us
  starting transfers between devices  110 us (47%)
  waiting for transfers between devices  55.8 us (24%)
  Pallas kernels  54.6 us (23%)
  other arithmetic  11.4 us (5%)
  local copies, waits for them, and re-layouts  3.47 us (1%)
    pallas_call x12, Pallas kernels, products(): pl.pallas_call(product_kernel, grid_spec=pltpu.PrefetchScalarGridSpec(num...  54.6 us
    ppermute x28, starting transfers between devices, swap(): return lax.ppermute(x, axis, [(0, 1), (1, 0)])  39.2 us
    ppermute x12, starting transfers between devices, chain(): two = lax.ppermute(sent, ('y', 'c'), flips(True))  33.2 us
    ppermute x12, starting transfers between devices, chain(): side = lax.ppermute(pair, ('z', 'c'), flips(True))  24.1 us
    ppermute x28, waiting for transfers between devices, swap(): return lax.ppermute(x, axis, [(0, 1), (1, 0)])  23.6 us
    ppermute x12, waiting for transfers between devices, chain(): two = lax.ppermute(sent, ('y', 'c'), flips(True))  13.7 us
    ppermute x12, starting transfers between devices, chain(): rest = lax.ppermute(four, ('z', 'c'), flips(False))  7.64 us
    ppermute x12, waiting for transfers between devices, chain(): one = lax.ppermute(p[:4 * u], ('y', 'c'), flips(False))  7.18 us
  transfers between devices with their start and end apart: 76, of which 36 were waited for; matrix products, arithmetic and copies ran while one was open for 5% of the time, Pallas kernels for 23%

profile of v2, /device:TPU:1, one launch (start us, length us, event | category | flops | bytes accessed | tf_op | source)
XLA Modules:
  0.0 235.7 jit_solution(4318521384404126562)
XLA Ops:
  12.9 3.8 %collective-permute-start.4 = (bf16[1024,128]{1,0:T(8,128)(2,1)S(1)}, bf16[1024,128]{1,0:T(8,128)(2,1)S(1)}, u32[]{:S(2)}, u32[]{:S(2)}) collective-permute-start(bf16[1024,128]{1,0:T(8,128)(2,1)S(1)} %pad_maximum_fusion.13), channel_id=1, source_target_pairs={{0,16},{1,49},{16,0},{17,33},{32,48},{33,17},{48,32},{49,1},{2,18}... | collective-permute-start | bytes 786440 | tf_op jit(solution)/shard_map/ppermute | solution.py:120
  31.3 4.6 %products.12 = bf16[4096,128]{1,0:T(8,128)(2,1)S(1)} custom-call(s32[16]{0:T(128)S(1)} %add.301.order, s32[256]{0:T(256)S(1)} %reshape.139.picks, bf16[64,2,128,128]{3,2,1,0:T(8,128)(2,1)S(1)} %broadcast_select_fusion.1.own, bf16[64,2,128,128]{3,2,1,0:T(8,128)(2,1)S(1)} %broadcast_select_fusion.other, bf16[2048,128]{1,0:T(8,128)(2,1)S(1)} %pad_maximum_fusion.refs_0_, ...), custom_call_target="tpu_custom_call" | custom-call | flops 536870912 | bytes 4194304 | tf_op jit(solution)/shard_map/products/pallas_call | solution.py:55
  39.8 4.5 %products.13 = bf16[4096,128]{1,0:T(8,128)(2,1)S(1)} custom-call(s32[16]{0:T(128)S(1)} %add.301.order, s32[256]{0:T(256)S(1)} %reshape.139.picks, bf16[64,2,128,128]{3,2,1,0:T(8,128)(2,1)S(1)} %broadcast_select_fusion.1.own, bf16[64,2,128,128]{3,2,1,0:T(8,128)(2,1)S(1)} %broadcast_select_fusion.other, bf16[2048,128]{1,0:T(8,128)(2,1)S(1)} %pad_maximum_fusion.1.refs_0_, ...), custom_call_target="tpu_custom_call" | custom-call | flops 536870912 | bytes 4194304 | tf_op jit(solution)/shard_map/products/pallas_call | solution.py:55
  49.9 4.5 %products.14 = bf16[4096,128]{1,0:T(8,128)(2,1)S(1)} custom-call(s32[16]{0:T(128)S(1)} %add.301.order, s32[256]{0:T(256)S(1)} %reshape.139.picks, bf16[64,2,128,128]{3,2,1,0:T(8,128)(2,1)S(1)} %broadcast_select_fusion.1.own, bf16[64,2,128,128]{3,2,1,0:T(8,128)(2,1)S(1)} %broadcast_select_fusion.other, bf16[2048,128]{1,0:T(8,128)(2,1)S(1)} %pad_maximum_fusion.3.refs_0_, ...), custom_call_target="tpu_custom_call" | custom-call | flops 536870912 | bytes 4194304 | tf_op jit(solution)/shard_map/products/pallas_call | solution.py:55
  60.5 4.5 %products.15 = bf16[4096,128]{1,0:T(8,128)(2,1)S(1)} custom-call(s32[16]{0:T(128)S(1)} %add.301.order, s32[256]{0:T(256)S(1)} %reshape.139.picks, bf16[64,2,128,128]{3,2,1,0:T(8,128)(2,1)S(1)} %broadcast_select_fusion.1.own, bf16[64,2,128,128]{3,2,1,0:T(8,128)(2,1)S(1)} %broadcast_select_fusion.other, bf16[2048,128]{1,0:T(8,128)(2,1)S(1)} %pad_maximum_fusion.2.refs_0_, ...), custom_call_target="tpu_custom_call" | custom-call | flops 536870912 | bytes 4194304 | tf_op jit(solution)/shard_map/products/pallas_call | solution.py:55
  72.6 3.7 %collective-permute-done.26 = bf16[2048,128]{1,0:T(8,128)(2,1)S(1)} collective-permute-done((bf16[2048,128]{1,0:T(8,128)(2,1)S(1)}, bf16[2048,128]{1,0:T(8,128)(2,1)S(1)}, u32[]{:S(2)}, u32[]{:S(2)}) %collective-permute-start.26) | collective-permute-done | bytes 524320 | tf_op jit(solution)/shard_map/ppermute | solution.py:124
  78.1 4.4 %collective-permute-start.30 = (bf16[1024,128]{1,0:T(8,128)(2,1)S(1)}, bf16[1024,128]{1,0:T(8,128)(2,1)S(1)}, u32[]{:S(2)}, u32[]{:S(2)}) collective-permute-start(bf16[1024,128]{1,0:T(8,128)(2,1)S(1)} %pad_maximum_fusion.18), channel_id=1, source_target_pairs={{0,16},{1,49},{16,0},{17,33},{32,48},{33,17},{48,32},{49,1},{2,18}... | collective-permute-start | bytes 786440 | tf_op jit(solution)/shard_map/ppermute | solution.py:120
  91.8 4.5 %products.16 = bf16[4096,128]{1,0:T(8,128)(2,1)S(1)} custom-call(s32[16]{0:T(128)S(1)} %add.301.order, s32[256]{0:T(256)S(1)} %reshape.139.picks, bf16[64,2,128,128]{3,2,1,0:T(8,128)(2,1)S(1)} %broadcast_select_fusion.1.own, bf16[64,2,128,128]{3,2,1,0:T(8,128)(2,1)S(1)} %broadcast_select_fusion.other, bf16[2048,128]{1,0:T(8,128)(2,1)S(1)} %pad_maximum_fusion.4.refs_0_, ...), custom_call_target="tpu_custom_call" | custom-call | flops 536870912 | bytes 4194304 | tf_op jit(solution)/shard_map/products/pallas_call | solution.py:55
  99.1 4.5 %products.17 = bf16[4096,128]{1,0:T(8,128)(2,1)S(1)} custom-call(s32[16]{0:T(128)S(1)} %add.301.order, s32[256]{0:T(256)S(1)} %reshape.139.picks, bf16[64,2,128,128]{3,2,1,0:T(8,128)(2,1)S(1)} %broadcast_select_fusion.1.own, bf16[64,2,128,128]{3,2,1,0:T(8,128)(2,1)S(1)} %broadcast_select_fusion.other, bf16[2048,128]{1,0:T(8,128)(2,1)S(1)} %pad_maximum_fusion.5.refs_0_, ...), custom_call_target="tpu_custom_call" | custom-call | flops 536870912 | bytes 4194304 | tf_op jit(solution)/shard_map/products/pallas_call | solution.py:55
  106.2 4.5 %collective-permute-start.37 = (bf16[1024,128]{1,0:T(8,128)(2,1)S(1)}, bf16[1024,128]{1,0:T(8,128)(2,1)S(1)}, u32[]{:S(2)}, u32[]{:S(2)}) collective-permute-start(bf16[1024,128]{1,0:T(8,128)(2,1)S(1)} %add_convert_fusion.7), channel_id=1, source_target_pairs={{0,4},{1,13},{4,0},{5,9},{8,12},{9,5},{12,8},{13,1},{2,6},{3,15},{... | collective-permute-start | bytes 786440 | tf_op jit(solution)/shard_map/ppermute | solution.py:126
  113.3 3.3 %collective-permute-start.42 = (bf16[1024,128]{1,0:T(8,128)(2,1)S(1)}, bf16[1024,128]{1,0:T(8,128)(2,1)S(1)}, u32[]{:S(2)}, u32[]{:S(2)}) collective-permute-start(bf16[1024,128]{1,0:T(8,128)(2,1)S(1)} %add_convert_fusion.6), channel_id=1, source_target_pairs={{0,4},{1,13},{4,0},{5,9},{8,12},{9,5},{12,8},{13,1},{2,6},{3,15},{... | collective-permute-start | bytes 786440 | tf_op jit(solution)/shard_map/ppermute | solution.py:126
  117.7 4.6 %products.18 = bf16[4096,128]{1,0:T(8,128)(2,1)S(1)} custom-call(s32[16]{0:T(128)S(1)} %add.301.order, s32[256]{0:T(256)S(1)} %reshape.139.picks, bf16[64,2,128,128]{3,2,1,0:T(8,128)(2,1)S(1)} %broadcast_select_fusion.1.own, bf16[64,2,128,128]{3,2,1,0:T(8,128)(2,1)S(1)} %broadcast_select_fusion.other, bf16[2048,128]{1,0:T(8,128)(2,1)S(1)} %pad_maximum_fusion.6.refs_0_, ...), custom_call_target="tpu_custom_call" | custom-call | flops 536870912 | bytes 4194304 | tf_op jit(solution)/shard_map/products/pallas_call | solution.py:55
  125.6 4.5 %products.19 = bf16[4096,128]{1,0:T(8,128)(2,1)S(1)} custom-call(s32[16]{0:T(128)S(1)} %add.301.order, s32[256]{0:T(256)S(1)} %reshape.139.picks, bf16[64,2,128,128]{3,2,1,0:T(8,128)(2,1)S(1)} %broadcast_select_fusion.1.own, bf16[64,2,128,128]{3,2,1,0:T(8,128)(2,1)S(1)} %broadcast_select_fusion.other, bf16[2048,128]{1,0:T(8,128)(2,1)S(1)} %pad_maximum_fusion.7.refs_0_, ...), custom_call_target="tpu_custom_call" | custom-call | flops 536870912 | bytes 4194304 | tf_op jit(solution)/shard_map/products/pallas_call | solution.py:55
  136.5 4.2 %collective-permute-start.49 = (bf16[1024,128]{1,0:T(8,128)(2,1)S(1)}, bf16[1024,128]{1,0:T(8,128)(2,1)S(1)}, u32[]{:S(2)}, u32[]{:S(2)}) collective-permute-start(bf16[1024,128]{1,0:T(8,128)(2,1)S(1)} %add_convert_fusion.5), channel_id=1, source_target_pairs={{0,4},{1,13},{4,0},{5,9},{8,12},{9,5},{12,8},{13,1},{2,6},{3,15},{... | collective-permute-start | bytes 786440 | tf_op jit(solution)/shard_map/ppermute | solution.py:126
  142.6 5.0 %collective-permute-done.49 = bf16[1024,128]{1,0:T(8,128)(2,1)S(1)} collective-permute-done((bf16[1024,128]{1,0:T(8,128)(2,1)S(1)}, bf16[1024,128]{1,0:T(8,128)(2,1)S(1)}, u32[]{:S(2)}, u32[]{:S(2)}) %collective-permute-start.49) | collective-permute-done | bytes 262176 | tf_op jit(solution)/shard_map/ppermute | solution.py:126
  161.7 4.5 %products.20 = bf16[4096,128]{1,0:T(8,128)(2,1)S(1)} custom-call(s32[16]{0:T(128)S(1)} %add.301.order, s32[256]{0:T(256)S(1)} %reshape.139.picks, bf16[64,2,128,128]{3,2,1,0:T(8,128)(2,1)S(1)} %broadcast_select_fusion.1.own, bf16[64,2,128,128]{3,2,1,0:T(8,128)(2,1)S(1)} %broadcast_select_fusion.other, bf16[2048,128]{1,0:T(8,128)(2,1)S(1)} %pad_maximum_fusion.8.refs_0_, ...), custom_call_target="tpu_custom_call" | custom-call | flops 536870912 | bytes 4194304 | tf_op jit(solution)/shard_map/products/pallas_call | solution.py:55
  169.2 4.5 %products.21 = bf16[4096,128]{1,0:T(8,128)(2,1)S(1)} custom-call(s32[16]{0:T(128)S(1)} %add.301.order, s32[256]{0:T(256)S(1)} %reshape.139.picks, bf16[64,2,128,128]{3,2,1,0:T(8,128)(2,1)S(1)} %broadcast_select_fusion.1.own, bf16[64,2,128,128]{3,2,1,0:T(8,128)(2,1)S(1)} %broadcast_select_fusion.other, bf16[2048,128]{1,0:T(8,128)(2,1)S(1)} %pad_maximum_fusion.9.refs_0_, ...), custom_call_target="tpu_custom_call" | custom-call | flops 536870912 | bytes 4194304 | tf_op jit(solution)/shard_map/products/pallas_call | solution.py:55
  179.6 4.5 %products.22 = bf16[4096,128]{1,0:T(8,128)(2,1)S(1)} custom-call(s32[16]{0:T(128)S(1)} %add.301.order, s32[256]{0:T(256)S(1)} %reshape.139.picks, bf16[64,2,128,128]{3,2,1,0:T(8,128)(2,1)S(1)} %broadcast_select_fusion.1.own, bf16[64,2,128,128]{3,2,1,0:T(8,128)(2,1)S(1)} %broadcast_select_fusion.other, bf16[2048,128]{1,0:T(8,128)(2,1)S(1)} %pad_maximum_fusion.11.refs_0_, ...), custom_call_target="tpu_custom_call" | custom-call | flops 536870912 | bytes 4194304 | tf_op jit(solution)/shard_map/products/pallas_call | solution.py:55
  184.4 3.7 %collective-permute-start.65 = (bf16[1024,128]{1,0:T(8,128)(2,1)S(1)}, bf16[1024,128]{1,0:T(8,128)(2,1)S(1)}, u32[]{:S(2)}, u32[]{:S(2)}) collective-permute-start(bf16[1024,128]{1,0:T(8,128)(2,1)S(1)} %add_convert_fusion.2), channel_id=1, source_target_pairs={{0,4},{1,13},{4,0},{5,9},{8,12},{9,5},{12,8},{13,1},{2,6},{3,15},{... | collective-permute-start | bytes 786440 | tf_op jit(solution)/shard_map/ppermute | solution.py:126
  188.1 4.5 %products.23 = bf16[4096,128]{1,0:T(8,128)(2,1)S(1)} custom-call(s32[16]{0:T(128)S(1)} %add.301.order, s32[256]{0:T(256)S(1)} %reshape.139.picks, bf16[64,2,128,128]{3,2,1,0:T(8,128)(2,1)S(1)} %broadcast_select_fusion.1.own, bf16[64,2,128,128]{3,2,1,0:T(8,128)(2,1)S(1)} %broadcast_select_fusion.other, bf16[2048,128]{1,0:T(8,128)(2,1)S(1)} %pad_maximum_fusion.10.refs_0_, ...), custom_call_target="tpu_custom_call" | custom-call | flops 536870912 | bytes 4194304 | tf_op jit(solution)/shard_map/products/pallas_call | solution.py:55
  202.6 4.8 %collective-permute-start.73 = (bf16[1024,128]{1,0:T(8,128)(2,1)S(1)}, bf16[1024,128]{1,0:T(8,128)(2,1)S(1)}, u32[]{:S(2)}, u32[]{:S(2)}) collective-permute-start(bf16[1024,128]{1,0:T(8,128)(2,1)S(1)} %add_convert_fusion), channel_id=1, source_target_pairs={{0,4},{1,13},{4,0},{5,9},{8,12},{9,5},{12,8},{13,1},{2,6},{3,15},{... | collective-permute-start | bytes 786440 | tf_op jit(solution)/shard_map/ppermute | solution.py:126
  208.4 6.0 %collective-permute-done.73 = bf16[1024,128]{1,0:T(8,128)(2,1)S(1)} collective-permute-done((bf16[1024,128]{1,0:T(8,128)(2,1)S(1)}, bf16[1024,128]{1,0:T(8,128)(2,1)S(1)}, u32[]{:S(2)}, u32[]{:S(2)}) %collective-permute-start.73) | collective-permute-done | bytes 262176 | tf_op jit(solution)/shard_map/ppermute | solution.py:126
  215.7 4.2 %collective-permute-done.74 = bf16[512,128]{1,0:T(8,128)(2,1)S(1)} collective-permute-done((bf16[512,128]{1,0:T(8,128)(2,1)S(1)}, bf16[512,128]{1,0:T(8,128)(2,1)S(1)}, u32[]{:S(2)}, u32[]{:S(2)}) %collective-permute-start.74) | collective-permute-done | bytes 131104 | tf_op jit(solution)/shard_map/ppermute | solution.py:23
  220.0 13.3 %collective-permute-start.75 = (bf16[4,256,128]{2,1,0:T(8,128)(2,1)S(1)}, bf16[4,256,128]{2,1,0:T(8,128)(2,1)S(1)}, u32[]{:S(2)}, u32[]{:S(2)}) collective-permute-start(bf16[4,256,128]{2,1,0:T(8,128)(2,1)S(1)} %get-tuple-element.160), channel_id=1, source_target_pairs={{0,1},{1,0},{2,3},{3,2},{4,5},{5,4},{6,7},{7,6},{8,9},{9,8},{10,11... | collective-permute-start | bytes 786440 | tf_op jit(solution)/shard_map/ppermute | solution.py:23
  (237 shorter events, 119.3 us)
Async XLA Ops:
  3.9 24.7 %collective-permute-start.2 = (bf16[64,2,128,128]{3,2,1,0:T(8,128)(2,1)}, bf16[64,2,128,128]{3,2,1,0:T(8,128)(2,1)}, u32[]{:S(2)}, u32[]{:S(2)}) collective-permute-start(bf16[64,2,128,128]{3,2,1,0:T(8,128)(2,1)} %bitcast.49), channel_id=1, source_target_pairs={{0,1},{1,0},{2,3},{3,2},{4,5},{5,4},{6,7},{7,6},{8,9},{9,8},{10,11... | collective-permute-start | bytes 12582920 | tf_op jit(solution)/shard_map/ppermute | solution.py:23
  24.2 15.6 %collective-permute-start.12 = (bf16[2048,128]{1,0:T(8,128)(2,1)S(1)}, bf16[2048,128]{1,0:T(8,128)(2,1)S(1)}, u32[]{:S(2)}, u32[]{:S(2)}) collective-permute-start(bf16[2048,128]{1,0:T(8,128)(2,1)S(1)} %pad_maximum_fusion.1.refs_0_), channel_id=1, source_target_pairs={{0,48},{1,17},{16,32},{17,1},{32,16},{33,49},{48,0},{49,33},{2,50}... | collective-permute-start | bytes 1572872 | tf_op jit(solution)/shard_map/ppermute | solution.py:122
  26.8 11.8 %collective-permute-start.13 = (bf16[1024,128]{1,0:T(8,128)(2,1)S(1)}, bf16[1024,128]{1,0:T(8,128)(2,1)S(1)}, u32[]{:S(2)}, u32[]{:S(2)}) collective-permute-start(bf16[1024,128]{1,0:T(8,128)(2,1)S(1)} %pad_maximum_fusion.15), channel_id=1, source_target_pairs={{0,16},{1,49},{16,0},{17,33},{32,48},{33,17},{48,32},{49,1},{2,18}... | collective-permute-start | bytes 786440 | tf_op jit(solution)/shard_map/ppermute | solution.py:120
  38.7 11.2 %collective-permute-start.15 = (bf16[2048,128]{1,0:T(8,128)(2,1)S(1)}, bf16[2048,128]{1,0:T(8,128)(2,1)S(1)}, u32[]{:S(2)}, u32[]{:S(2)}) collective-permute-start(bf16[2048,128]{1,0:T(8,128)(2,1)S(1)} %pad_maximum_fusion.3.refs_0_), channel_id=1, source_target_pairs={{0,48},{1,17},{16,32},{17,1},{32,16},{33,49},{48,0},{49,33},{2,50}... | collective-permute-start | bytes 1572872 | tf_op jit(solution)/shard_map/ppermute | solution.py:122
  44.4 13.2 %collective-permute-start.18 = (bf16[2048,128]{1,0:T(8,128)(2,1)S(1)}, bf16[2048,128]{1,0:T(8,128)(2,1)S(1)}, u32[]{:S(2)}, u32[]{:S(2)}) collective-permute-start(bf16[2048,128]{1,0:T(8,128)(2,1)S(1)} %slice.356), channel_id=1, source_target_pairs={{0,12},{1,5},{4,8},{5,1},{8,4},{9,13},{12,0},{13,9},{2,14},{3,7},{... | collective-permute-start | bytes 1572872 | tf_op jit(solution)/shard_map/ppermute | solution.py:124
  48.5 12.0 %collective-permute-start.17 = (bf16[2048,128]{1,0:T(8,128)(2,1)S(1)}, bf16[2048,128]{1,0:T(8,128)(2,1)S(1)}, u32[]{:S(2)}, u32[]{:S(2)}) collective-permute-start(bf16[2048,128]{1,0:T(8,128)(2,1)S(1)} %pad_maximum_fusion.2.refs_0_), channel_id=1, source_target_pairs={{0,48},{1,17},{16,32},{17,1},{32,16},{33,49},{48,0},{49,33},{2,50}... | collective-permute-start | bytes 1572872 | tf_op jit(solution)/shard_map/ppermute | solution.py:122
  54.5 13.1 %collective-permute-start.20 = (bf16[2048,128]{1,0:T(8,128)(2,1)S(1)}, bf16[2048,128]{1,0:T(8,128)(2,1)S(1)}, u32[]{:S(2)}, u32[]{:S(2)}) collective-permute-start(bf16[2048,128]{1,0:T(8,128)(2,1)S(1)} %slice.359), channel_id=1, source_target_pairs={{0,12},{1,5},{4,8},{5,1},{8,4},{9,13},{12,0},{13,9},{2,14},{3,7},{... | collective-permute-start | bytes 1572872 | tf_op jit(solution)/shard_map/ppermute | solution.py:124
  65.1 11.2 %collective-permute-start.26 = (bf16[2048,128]{1,0:T(8,128)(2,1)S(1)}, bf16[2048,128]{1,0:T(8,128)(2,1)S(1)}, u32[]{:S(2)}, u32[]{:S(2)}) collective-permute-start(bf16[2048,128]{1,0:T(8,128)(2,1)S(1)} %slice.371), channel_id=1, source_target_pairs={{0,12},{1,5},{4,8},{5,1},{8,4},{9,13},{12,0},{13,9},{2,14},{3,7},{... | collective-permute-start | bytes 1572872 | tf_op jit(solution)/shard_map/ppermute | solution.py:124
  69.8 12.8 %collective-permute-start.22 = (bf16[1024,128]{1,0:T(8,128)(2,1)S(1)}, bf16[1024,128]{1,0:T(8,128)(2,1)S(1)}, u32[]{:S(2)}, u32[]{:S(2)}) collective-permute-start(bf16[1024,128]{1,0:T(8,128)(2,1)S(1)} %pad_maximum_fusion.17), channel_id=1, source_target_pairs={{0,16},{1,49},{16,0},{17,33},{32,48},{33,17},{48,32},{49,1},{2,18}... | collective-permute-start | bytes 786440 | tf_op jit(solution)/shard_map/ppermute | solution.py:120
  84.1 12.4 %collective-permute-start.33 = (bf16[512,128]{1,0:T(8,128)(2,1)S(1)}, bf16[512,128]{1,0:T(8,128)(2,1)S(1)}, u32[]{:S(2)}, u32[]{:S(2)}) collective-permute-start(bf16[512,128]{1,0:T(8,128)(2,1)S(1)} %add_convert_fusion.20), channel_id=1, source_target_pairs={{0,64},{64,0},{1,65},{65,1},{2,66},{66,2},{3,67},{67,3},{4,68},{68... | collective-permute-start | bytes 393224 | tf_op jit(solution)/shard_map/ppermute | solution.py:23
  86.4 12.8 %collective-permute-start.36 = (bf16[2048,128]{1,0:T(8,128)(2,1)S(1)}, bf16[2048,128]{1,0:T(8,128)(2,1)S(1)}, u32[]{:S(2)}, u32[]{:S(2)}) collective-permute-start(bf16[2048,128]{1,0:T(8,128)(2,1)S(1)} %pad_maximum_fusion.5.refs_0_), channel_id=1, source_target_pairs={{0,48},{1,17},{16,32},{17,1},{32,16},{33,49},{48,0},{49,33},{2,50}... | collective-permute-start | bytes 1572872 | tf_op jit(solution)/shard_map/ppermute | solution.py:122
  105.9 11.7 %collective-permute-start.38 = (bf16[2048,128]{1,0:T(8,128)(2,1)S(1)}, bf16[2048,128]{1,0:T(8,128)(2,1)S(1)}, u32[]{:S(2)}, u32[]{:S(2)}) collective-permute-start(bf16[2048,128]{1,0:T(8,128)(2,1)S(1)} %pad_maximum_fusion.6.refs_0_), channel_id=1, source_target_pairs={{0,48},{1,17},{16,32},{17,1},{32,16},{33,49},{48,0},{49,33},{2,50}... | collective-permute-start | bytes 1572872 | tf_op jit(solution)/shard_map/ppermute | solution.py:122
  106.2 11.4 %collective-permute-start.37 = (bf16[1024,128]{1,0:T(8,128)(2,1)S(1)}, bf16[1024,128]{1,0:T(8,128)(2,1)S(1)}, u32[]{:S(2)}, u32[]{:S(2)}) collective-permute-start(bf16[1024,128]{1,0:T(8,128)(2,1)S(1)} %add_convert_fusion.7), channel_id=1, source_target_pairs={{0,4},{1,13},{4,0},{5,9},{8,12},{9,5},{12,8},{13,1},{2,6},{3,15},{... | collective-permute-start | bytes 786440 | tf_op jit(solution)/shard_map/ppermute | solution.py:126
  111.8 13.8 %collective-permute-start.43 = (bf16[2048,128]{1,0:T(8,128)(2,1)S(1)}, bf16[2048,128]{1,0:T(8,128)(2,1)S(1)}, u32[]{:S(2)}, u32[]{:S(2)}) collective-permute-start(bf16[2048,128]{1,0:T(8,128)(2,1)S(1)} %pad_maximum_fusion.7.refs_0_), channel_id=1, source_target_pairs={{0,48},{1,17},{16,32},{17,1},{32,16},{33,49},{48,0},{49,33},{2,50}... | collective-permute-start | bytes 1572872 | tf_op jit(solution)/shard_map/ppermute | solution.py:122
  123.4 12.2 %collective-permute-start.46 = (bf16[2048,128]{1,0:T(8,128)(2,1)S(1)}, bf16[2048,128]{1,0:T(8,128)(2,1)S(1)}, u32[]{:S(2)}, u32[]{:S(2)}) collective-permute-start(bf16[2048,128]{1,0:T(8,128)(2,1)S(1)} %slice.401), channel_id=1, source_target_pairs={{0,12},{1,5},{4,8},{5,1},{8,4},{9,13},{12,0},{13,9},{2,14},{3,7},{... | collective-permute-start | bytes 1572872 | tf_op jit(solution)/shard_map/ppermute | solution.py:124
  141.9 11.4 %collective-permute-start.53 = (bf16[1024,128]{1,0:T(8,128)(2,1)S(1)}, bf16[1024,128]{1,0:T(8,128)(2,1)S(1)}, u32[]{:S(2)}, u32[]{:S(2)}) collective-permute-start(bf16[1024,128]{1,0:T(8,128)(2,1)S(1)} %add_convert_fusion.4), channel_id=1, source_target_pairs={{0,4},{1,13},{4,0},{5,9},{8,12},{9,5},{12,8},{13,1},{2,6},{3,15},{... | collective-permute-start | bytes 786440 | tf_op jit(solution)/shard_map/ppermute | solution.py:126
  150.2 11.5 %collective-permute-start.51 = (bf16[2048,128]{1,0:T(8,128)(2,1)S(1)}, bf16[2048,128]{1,0:T(8,128)(2,1)S(1)}, u32[]{:S(2)}, u32[]{:S(2)}) collective-permute-start(bf16[2048,128]{1,0:T(8,128)(2,1)S(1)} %pad_maximum_fusion.8.refs_0_), channel_id=1, source_target_pairs={{0,48},{1,17},{16,32},{17,1},{32,16},{33,49},{48,0},{49,33},{2,50}... | collective-permute-start | bytes 1572872 | tf_op jit(solution)/shard_map/ppermute | solution.py:122
  155.2 14.0 %collective-permute-start.60 = (bf16[2048,128]{1,0:T(8,128)(2,1)S(1)}, bf16[2048,128]{1,0:T(8,128)(2,1)S(1)}, u32[]{:S(2)}, u32[]{:S(2)}) collective-permute-start(bf16[2048,128]{1,0:T(8,128)(2,1)S(1)} %pad_maximum_fusion.9.refs_0_), channel_id=1, source_target_pairs={{0,48},{1,17},{16,32},{17,1},{32,16},{33,49},{48,0},{49,33},{2,50}... | collective-permute-start | bytes 1572872 | tf_op jit(solution)/shard_map/ppermute | solution.py:122
  168.1 11.5 %collective-permute-start.64 = (bf16[2048,128]{1,0:T(8,128)(2,1)S(1)}, bf16[2048,128]{1,0:T(8,128)(2,1)S(1)}, u32[]{:S(2)}, u32[]{:S(2)}) collective-permute-start(bf16[2048,128]{1,0:T(8,128)(2,1)S(1)} %pad_maximum_fusion.11.refs_0_), channel_id=1, source_target_pairs={{0,48},{1,17},{16,32},{17,1},{32,16},{33,49},{48,0},{49,33},{2,50}... | collective-permute-start | bytes 1572872 | tf_op jit(solution)/shard_map/ppermute | solution.py:122
  176.1 12.0 %collective-permute-start.66 = (bf16[2048,128]{1,0:T(8,128)(2,1)S(1)}, bf16[2048,128]{1,0:T(8,128)(2,1)S(1)}, u32[]{:S(2)}, u32[]{:S(2)}) collective-permute-start(bf16[2048,128]{1,0:T(8,128)(2,1)S(1)} %pad_maximum_fusion.10.refs_0_), channel_id=1, source_target_pairs={{0,48},{1,17},{16,32},{17,1},{32,16},{33,49},{48,0},{49,33},{2,50}... | collective-permute-start | bytes 1572872 | tf_op jit(solution)/shard_map/ppermute | solution.py:122
  176.4 17.2 %collective-permute-start.62 = (bf16[1024,128]{1,0:T(8,128)(2,1)S(1)}, bf16[1024,128]{1,0:T(8,128)(2,1)S(1)}, u32[]{:S(2)}, u32[]{:S(2)}) collective-permute-start(bf16[1024,128]{1,0:T(8,128)(2,1)S(1)} %add_convert_fusion.3), channel_id=1, source_target_pairs={{0,4},{1,13},{4,0},{5,9},{8,12},{9,5},{12,8},{13,1},{2,6},{3,15},{... | collective-permute-start | bytes 786440 | tf_op jit(solution)/shard_map/ppermute | solution.py:126
  184.2 14.0 %collective-permute-start.69 = (bf16[2048,128]{1,0:T(8,128)(2,1)S(1)}, bf16[2048,128]{1,0:T(8,128)(2,1)S(1)}, u32[]{:S(2)}, u32[]{:S(2)}) collective-permute-start(bf16[2048,128]{1,0:T(8,128)(2,1)S(1)} %slice.437), channel_id=1, source_target_pairs={{0,12},{1,5},{4,8},{5,1},{8,4},{9,13},{12,0},{13,9},{2,14},{3,7},{... | collective-permute-start | bytes 1572872 | tf_op jit(solution)/shard_map/ppermute | solution.py:124
  202.6 11.8 %collective-permute-start.73 = (bf16[1024,128]{1,0:T(8,128)(2,1)S(1)}, bf16[1024,128]{1,0:T(8,128)(2,1)S(1)}, u32[]{:S(2)}, u32[]{:S(2)}) collective-permute-start(bf16[1024,128]{1,0:T(8,128)(2,1)S(1)} %add_convert_fusion), channel_id=1, source_target_pairs={{0,4},{1,13},{4,0},{5,9},{8,12},{9,5},{12,8},{13,1},{2,6},{3,15},{... | collective-permute-start | bytes 786440 | tf_op jit(solution)/shard_map/ppermute | solution.py:126
  220.0 14.5 %collective-permute-start.75 = (bf16[4,256,128]{2,1,0:T(8,128)(2,1)S(1)}, bf16[4,256,128]{2,1,0:T(8,128)(2,1)S(1)}, u32[]{:S(2)}, u32[]{:S(2)}) collective-permute-start(bf16[4,256,128]{2,1,0:T(8,128)(2,1)S(1)} %get-tuple-element.160), channel_id=1, source_target_pairs={{0,1},{1,0},{2,3},{3,2},{4,5},{5,4},{6,7},{7,6},{8,9},{9,8},{10,11... | collective-permute-start | bytes 786440 | tf_op jit(solution)/shard_map/ppermute | solution.py:23
  (52 other events, 395.1 us)

commit v3 on v2

--- a/solution.py
+++ b/solution.py
@@ -91,24 +91,26 @@
     own, first = lax.optimization_barrier((own, first))
     other = swap(own, "c")
 
-    r, i = tile_col[:, 0] // 4, tile_col[:, 0] % 4
-    dx, dz = (r // 4) ^ xl, (r & 3) ^ z
-    live = jnp.arange(2, dtype=jnp.int32)[None, :] < tile_count
+    def prepare(tile_col, tile_count, y, xh, c, own, other):
+        r, i = tile_col[:, 0] // 4, tile_col[:, 0] % 4
+        dx, dz = (r // 4) ^ xl, (r & 3) ^ z
+        live = jnp.arange(2, dtype=jnp.int32)[None, :] < tile_count
 
-    def code(core, shift):
-        slot = jnp.where(dz == 0, 0, jnp.where(dz == 2, 3, jnp.where(dz == 1 + 2 * core, 1, 2)))
-        return jnp.where(live, (slot * 2 + dx) * UNIT + shift + i, 8 * UNIT)
+        def code(core, shift):
+            slot = jnp.where(dz == 0, 0, jnp.where(dz == 2, 3, jnp.where(dz == 1 + 2 * core, 1, 2)))
+            return jnp.where(live, (slot * 2 + dx) * UNIT + shift + i, 8 * UNIT)
 
-    codes = code(c, 0), swap(code(1 - c, 4), "c")
-    picks = jnp.concatenate(codes, axis=1).reshape(-1)
-    own, other = (
-        jnp.where((at < 8 * UNIT)[:, :, None, None], t, jnp.zeros((), t.dtype)) for at, t in zip(codes, (own, other))
-    )
+        codes = code(c, 0), swap(code(1 - c, 4), "c")
+        picks = jnp.concatenate(codes, axis=1).reshape(-1)
+        own, other = (
+            jnp.where((at < 8 * UNIT)[:, :, None, None], t, jnp.zeros((), t.dtype)) for at, t in zip(codes, (own, other))
+        )
 
-    far, near = 3 - 2 * c, 1 + 2 * c
-    dy = jnp.stack([far, far, jnp.int32(2), jnp.int32(2), near, near, jnp.int32(0), jnp.int32(0)])
-    unit = (y ^ dy) * 2 + (xh ^ np.array([1, 0] * 4, np.int32))
-    order = ((unit * 2)[:, None] + (c ^ np.array([[0, 1]], np.int32))).reshape(-1).astype(jnp.int32)
+        far, near = 3 - 2 * c, 1 + 2 * c
+        dy = jnp.stack([far, far, jnp.int32(2), jnp.int32(2), near, near, jnp.int32(0), jnp.int32(0)])
+        unit = (y ^ dy) * 2 + (xh ^ np.array([1, 0] * 4, np.int32))
+        order = ((unit * 2)[:, None] + (c ^ np.array([[0, 1]], np.int32))).reshape(-1).astype(jnp.int32)
+        return order, picks, own, other
 
     def chain(v):
         previous = None
@@ -120,7 +122,7 @@
             side = lax.ppermute(pair, ("z", "c"), flips(True))
             four = yield jnp.concatenate([pair, side], axis=0)
             rest = lax.ppermute(four, ("z", "c"), flips(False))
-            p = yield products(order, picks, own, other, (four, rest))
+            p = yield products(*prepared, (four, rest))
             one = lax.ppermute(p[: 4 * u], ("y", "c"), flips(False))
             sent = yield add(p[4 * u : 6 * u], one[2 * u :]).astype(p.dtype)
             two = lax.ppermute(sent, ("y", "c"), flips(True))
@@ -134,16 +136,20 @@
 
     chains = [chain(v) for v in first]
     waiting = [next(steps) for steps in chains]
-    last = None
-    for k in TURNS:
+    last, prepared = None, []
+    for turn, k in enumerate(TURNS):
         if last is None:
             last = waiting[k]
         else:
             last, _ = lax.optimization_barrier((waiting[k], last))
+        if turn == 2:
+            tied = lax.optimization_barrier((tile_col, tile_count, y, xh, c, last))
+            prepared = prepare(*tied[:5], own, other)
         waiting[k] = chains[k].send(last)
 
-    done = jnp.concatenate([v.reshape(2 * rows // BLK, -1, BLK) for v in waiting], axis=1)
-    kept, got = done[: rows // BLK], swap(done[rows // BLK :], "c")
+    done = [v.reshape(2 * rows // BLK, -1, BLK) for v in waiting]
+    kept = jnp.concatenate([v[: rows // BLK] for v in done], axis=1)
+    got = jnp.concatenate([swap(v[rows // BLK :], "c") for v in done], axis=1)
     turned = jnp.where(c == 0, jnp.concatenate([kept, got], axis=1), jnp.concatenate([got, kept], axis=1))
     return turned.transpose(0, 2, 1).reshape(rows, 2 * half)
 

time: 236 us -> 244 us (1.034)
  other arithmetic: 11.4 us -> 16.9 us
  starting transfers between devices: 110 us -> 114 us
  waiting for transfers between devices: 55.8 us -> 52.5 us
    ppermute x28 -> x31, starting transfers between devices: 39.2 us -> 54.9 us  [swap(): return lax.ppermute(x, axis, [(0, 1), (1, 0)])]
    ppermute x12, waiting for transfers between devices: 7.18 us -> 0.39 us  [chain(): one = lax.ppermute(p[:4 * u], ('y', 'c'), flips(False))]
    ppermute x12, waiting for transfers between devices: 4.56 us -> 11 us  [chain(): side = lax.ppermute(pair, ('z', 'c'), flips(True))]
    ppermute x12, starting transfers between devices: 33.2 us -> 27.2 us  [chain(): two = lax.ppermute(sent, ('y', 'c'), flips(True))]
    ppermute x12, starting transfers between devices: 24.1 us -> 19.7 us  [chain(): side = lax.ppermute(pair, ('z', 'c'), flips(True))]
    ppermute x12, starting transfers between devices: 7.64 us -> 3.96 us  [chain(): rest = lax.ppermute(four, ('z', 'c'), flips(False))]
    ppermute x12, waiting for transfers between devices: 13.7 us -> 10.4 us  [chain(): two = lax.ppermute(sent, ('y', 'c'), flips(True))]
    ppermute x12, starting transfers between devices: 5.52 us -> 8.71 us  [chain(): one = lax.ppermute(p[:4 * u], ('y', 'c'), flips(False))]
  transfers between devices with their start and end apart: 76 -> 79, of which waited for: 36 -> 35; matrix products, arithmetic and copies ran while one was open for 5% -> 7% of each run, Pallas kernels for 23% -> 22%
where the time goes in v3:
time: 244 us
  starting transfers between devices  114 us (47%)
  Pallas kernels  54.6 us (22%)
  waiting for transfers between devices  52.5 us (22%)
  other arithmetic  16.9 us (7%)
  local copies, waits for them, and re-layouts  4.46 us (2%)
    ppermute x31, starting transfers between devices, swap(): return lax.ppermute(x, axis, [(0, 1), (1, 0)])  54.9 us
    pallas_call x12, Pallas kernels, products(): pl.pallas_call(product_kernel, grid_spec=pltpu.PrefetchScalarGridSpec(num...  54.6 us
    ppermute x12, starting transfers between devices, chain(): two = lax.ppermute(sent, ('y', 'c'), flips(True))  27.2 us
    ppermute x31, waiting for transfers between devices, swap(): return lax.ppermute(x, axis, [(0, 1), (1, 0)])  22.8 us
    ppermute x12, starting transfers between devices, chain(): side = lax.ppermute(pair, ('z', 'c'), flips(True))  19.7 us
    ppermute x12, waiting for transfers between devices, chain(): side = lax.ppermute(pair, ('z', 'c'), flips(True))  11 us
    ppermute x12, waiting for transfers between devices, chain(): two = lax.ppermute(sent, ('y', 'c'), flips(True))  10.4 us
    ppermute x12, starting transfers between devices, chain(): one = lax.ppermute(p[:4 * u], ('y', 'c'), flips(False))  8.71 us
  transfers between devices with their start and end apart: 79, of which 35 were waited for; matrix products, arithmetic and copies ran while one was open for 7% of the time, Pallas kernels for 22%

profile of v3, /device:TPU:1, one launch (start us, length us, event | category | flops | bytes accessed | tf_op | source)
XLA Modules:
  0.0 243.9 jit_solution(4556174134448210855)
XLA Ops:
  5.9 3.5 %collective-permute-done.1 = bf16[512,128]{1,0:T(8,128)(2,1)S(1)} collective-permute-done((bf16[512,128]{1,0:T(8,128)(2,1)S(1)}, bf16[512,128]{1,0:T(8,128)(2,1)S(1)}, u32[]{:S(2)}, u32[]{:S(2)}) %collective-permute-start.1) | collective-permute-done | bytes 131104 | tf_op jit(solution)/shard_map/ppermute | solution.py:23
  9.4 3.9 %collective-permute-start.4 = (bf16[1024,128]{1,0:T(8,128)(2,1)S(1)}, bf16[1024,128]{1,0:T(8,128)(2,1)S(1)}, u32[]{:S(2)}, u32[]{:S(2)}) collective-permute-start(bf16[1024,128]{1,0:T(8,128)(2,1)S(1)} %pad_maximum_fusion.12), channel_id=1, source_target_pairs={{0,16},{1,49},{16,0},{17,33},{32,48},{33,17},{48,32},{49,1},{2,18}... | collective-permute-start | bytes 786440 | tf_op jit(solution)/shard_map/ppermute | solution.py:122
  16.4 4.6 %broadcast_select_fusion.1.own = bf16[64,2,128,128]{3,2,1,0:T(8,128)(2,1)} fusion(bf16[64,2,128,128]{3,2,1,0:T(8,128)(2,1)} %bitcast.54, pred[64,2]{1,0:T(8,128)(4,1)S(1)} %copy.15), kind=kLoop, calls=%fused_computation.1 | loop fusion | flops 2097152 | bytes 8388736 | tf_op jit(solution)/shard_map/jit(_where)/select_n | solution.py:106
  25.7 3.4 %collective-permute-done.8 = bf16[1024,128]{1,0:T(8,128)(2,1)S(1)} collective-permute-done((bf16[1024,128]{1,0:T(8,128)(2,1)S(1)}, bf16[1024,128]{1,0:T(8,128)(2,1)S(1)}, u32[]{:S(2)}, u32[]{:S(2)}) %collective-permute-start.8) | collective-permute-done | bytes 262176 | tf_op jit(solution)/shard_map/ppermute | solution.py:122
  35.0 4.5 %products.12 = bf16[4096,128]{1,0:T(8,128)(2,1)S(1)} custom-call(s32[16]{0:T(128)S(1)} %add.303.order, s32[256]{0:T(256)S(1)} %reshape.144.picks, bf16[64,2,128,128]{3,2,1,0:T(8,128)(2,1)S(1)} %copy-done, bf16[64,2,128,128]{3,2,1,0:T(8,128)(2,1)S(1)} %broadcast_select_fusion.other, bf16[2048,128]{1,0:T(8,128)(2,1)S(1)} %pad_maximum_fusion.refs_0_, ...), custom_call_target="tpu_custom_call" | custom-call | flops 536870912 | bytes 4194304 | tf_op jit(solution)/shard_map/products/pallas_call | solution.py:55
  42.5 4.5 %products.13 = bf16[4096,128]{1,0:T(8,128)(2,1)S(1)} custom-call(s32[16]{0:T(128)S(1)} %add.303.order, s32[256]{0:T(256)S(1)} %reshape.144.picks, bf16[64,2,128,128]{3,2,1,0:T(8,128)(2,1)S(1)} %copy-done, bf16[64,2,128,128]{3,2,1,0:T(8,128)(2,1)S(1)} %broadcast_select_fusion.other, bf16[2048,128]{1,0:T(8,128)(2,1)S(1)} %pad_maximum_fusion.1.refs_0_, ...), custom_call_target="tpu_custom_call" | custom-call | flops 536870912 | bytes 4194304 | tf_op jit(solution)/shard_map/products/pallas_call | solution.py:55
  52.5 4.5 %products.14 = bf16[4096,128]{1,0:T(8,128)(2,1)S(1)} custom-call(s32[16]{0:T(128)S(1)} %add.303.order, s32[256]{0:T(256)S(1)} %reshape.144.picks, bf16[64,2,128,128]{3,2,1,0:T(8,128)(2,1)S(1)} %copy-done, bf16[64,2,128,128]{3,2,1,0:T(8,128)(2,1)S(1)} %broadcast_select_fusion.other, bf16[2048,128]{1,0:T(8,128)(2,1)S(1)} %pad_maximum_fusion.3.refs_0_, ...), custom_call_target="tpu_custom_call" | custom-call | flops 536870912 | bytes 4194304 | tf_op jit(solution)/shard_map/products/pallas_call | solution.py:55
  60.6 3.1 %collective-permute-start.21 = (bf16[1024,128]{1,0:T(8,128)(2,1)S(1)}, bf16[1024,128]{1,0:T(8,128)(2,1)S(1)}, u32[]{:S(2)}, u32[]{:S(2)}) collective-permute-start(bf16[1024,128]{1,0:T(8,128)(2,1)S(1)} %add_convert_fusion.10), channel_id=1, source_target_pairs={{0,4},{1,13},{4,0},{5,9},{8,12},{9,5},{12,8},{13,1},{2,6},{3,15},{... | collective-permute-start | bytes 786440 | tf_op jit(solution)/shard_map/ppermute | solution.py:128
  63.7 4.5 %products.15 = bf16[4096,128]{1,0:T(8,128)(2,1)S(1)} custom-call(s32[16]{0:T(128)S(1)} %add.303.order, s32[256]{0:T(256)S(1)} %reshape.144.picks, bf16[64,2,128,128]{3,2,1,0:T(8,128)(2,1)S(1)} %copy-done, bf16[64,2,128,128]{3,2,1,0:T(8,128)(2,1)S(1)} %broadcast_select_fusion.other, bf16[2048,128]{1,0:T(8,128)(2,1)S(1)} %pad_maximum_fusion.2.refs_0_, ...), custom_call_target="tpu_custom_call" | custom-call | flops 536870912 | bytes 4194304 | tf_op jit(solution)/shard_map/products/pallas_call | solution.py:55
  76.8 4.0 %collective-permute-start.28 = (bf16[1024,128]{1,0:T(8,128)(2,1)S(1)}, bf16[1024,128]{1,0:T(8,128)(2,1)S(1)}, u32[]{:S(2)}, u32[]{:S(2)}) collective-permute-start(bf16[1024,128]{1,0:T(8,128)(2,1)S(1)} %add_convert_fusion.8), channel_id=1, source_target_pairs={{0,4},{1,13},{4,0},{5,9},{8,12},{9,5},{12,8},{13,1},{2,6},{3,15},{... | collective-permute-start | bytes 786440 | tf_op jit(solution)/shard_map/ppermute | solution.py:128
  95.6 4.5 %products.16 = bf16[4096,128]{1,0:T(8,128)(2,1)S(1)} custom-call(s32[16]{0:T(128)S(1)} %add.303.order, s32[256]{0:T(256)S(1)} %reshape.144.picks, bf16[64,2,128,128]{3,2,1,0:T(8,128)(2,1)S(1)} %copy-done, bf16[64,2,128,128]{3,2,1,0:T(8,128)(2,1)S(1)} %broadcast_select_fusion.other, bf16[2048,128]{1,0:T(8,128)(2,1)S(1)} %pad_maximum_fusion.4.refs_0_, ...), custom_call_target="tpu_custom_call" | custom-call | flops 536870912 | bytes 4194304 | tf_op jit(solution)/shard_map/products/pallas_call | solution.py:55
  102.5 4.6 %products.17 = bf16[4096,128]{1,0:T(8,128)(2,1)S(1)} custom-call(s32[16]{0:T(128)S(1)} %add.303.order, s32[256]{0:T(256)S(1)} %reshape.144.picks, bf16[64,2,128,128]{3,2,1,0:T(8,128)(2,1)S(1)} %copy-done, bf16[64,2,128,128]{3,2,1,0:T(8,128)(2,1)S(1)} %broadcast_select_fusion.other, bf16[2048,128]{1,0:T(8,128)(2,1)S(1)} %pad_maximum_fusion.5.refs_0_, ...), custom_call_target="tpu_custom_call" | custom-call | flops 536870912 | bytes 4194304 | tf_op jit(solution)/shard_map/products/pallas_call | solution.py:55
  112.2 3.1 %collective-permute-done.40 = bf16[1024,128]{1,0:T(8,128)(2,1)S(1)} collective-permute-done((bf16[1024,128]{1,0:T(8,128)(2,1)S(1)}, bf16[1024,128]{1,0:T(8,128)(2,1)S(1)}, u32[]{:S(2)}, u32[]{:S(2)}) %collective-permute-start.40) | collective-permute-done | bytes 262176 | tf_op jit(solution)/shard_map/ppermute | solution.py:122
  119.3 4.5 %products.18 = bf16[4096,128]{1,0:T(8,128)(2,1)S(1)} custom-call(s32[16]{0:T(128)S(1)} %add.303.order, s32[256]{0:T(256)S(1)} %reshape.144.picks, bf16[64,2,128,128]{3,2,1,0:T(8,128)(2,1)S(1)} %copy-done, bf16[64,2,128,128]{3,2,1,0:T(8,128)(2,1)S(1)} %broadcast_select_fusion.other, bf16[2048,128]{1,0:T(8,128)(2,1)S(1)} %pad_maximum_fusion.6.refs_0_, ...), custom_call_target="tpu_custom_call" | custom-call | flops 536870912 | bytes 4194304 | tf_op jit(solution)/shard_map/products/pallas_call | solution.py:55
  128.0 4.5 %products.19 = bf16[4096,128]{1,0:T(8,128)(2,1)S(1)} custom-call(s32[16]{0:T(128)S(1)} %add.303.order, s32[256]{0:T(256)S(1)} %reshape.144.picks, bf16[64,2,128,128]{3,2,1,0:T(8,128)(2,1)S(1)} %copy-done, bf16[64,2,128,128]{3,2,1,0:T(8,128)(2,1)S(1)} %broadcast_select_fusion.other, bf16[2048,128]{1,0:T(8,128)(2,1)S(1)} %pad_maximum_fusion.7.refs_0_, ...), custom_call_target="tpu_custom_call" | custom-call | flops 536870912 | bytes 4194304 | tf_op jit(solution)/shard_map/products/pallas_call | solution.py:55
  163.3 4.5 %products.20 = bf16[4096,128]{1,0:T(8,128)(2,1)S(1)} custom-call(s32[16]{0:T(128)S(1)} %add.303.order, s32[256]{0:T(256)S(1)} %reshape.144.picks, bf16[64,2,128,128]{3,2,1,0:T(8,128)(2,1)S(1)} %copy-done, bf16[64,2,128,128]{3,2,1,0:T(8,128)(2,1)S(1)} %broadcast_select_fusion.other, bf16[2048,128]{1,0:T(8,128)(2,1)S(1)} %pad_maximum_fusion.8.refs_0_, ...), custom_call_target="tpu_custom_call" | custom-call | flops 536870912 | bytes 4194304 | tf_op jit(solution)/shard_map/products/pallas_call | solution.py:55
  170.6 4.5 %products.21 = bf16[4096,128]{1,0:T(8,128)(2,1)S(1)} custom-call(s32[16]{0:T(128)S(1)} %add.303.order, s32[256]{0:T(256)S(1)} %reshape.144.picks, bf16[64,2,128,128]{3,2,1,0:T(8,128)(2,1)S(1)} %copy-done, bf16[64,2,128,128]{3,2,1,0:T(8,128)(2,1)S(1)} %broadcast_select_fusion.other, bf16[2048,128]{1,0:T(8,128)(2,1)S(1)} %pad_maximum_fusion.9.refs_0_, ...), custom_call_target="tpu_custom_call" | custom-call | flops 536870912 | bytes 4194304 | tf_op jit(solution)/shard_map/products/pallas_call | solution.py:55
  181.0 4.5 %products.22 = bf16[4096,128]{1,0:T(8,128)(2,1)S(1)} custom-call(s32[16]{0:T(128)S(1)} %add.303.order, s32[256]{0:T(256)S(1)} %reshape.144.picks, bf16[64,2,128,128]{3,2,1,0:T(8,128)(2,1)S(1)} %copy-done, bf16[64,2,128,128]{3,2,1,0:T(8,128)(2,1)S(1)} %broadcast_select_fusion.other, bf16[2048,128]{1,0:T(8,128)(2,1)S(1)} %pad_maximum_fusion.11.refs_0_, ...), custom_call_target="tpu_custom_call" | custom-call | flops 536870912 | bytes 4194304 | tf_op jit(solution)/shard_map/products/pallas_call | solution.py:55
  189.6 4.5 %products.23 = bf16[4096,128]{1,0:T(8,128)(2,1)S(1)} custom-call(s32[16]{0:T(128)S(1)} %add.303.order, s32[256]{0:T(256)S(1)} %reshape.144.picks, bf16[64,2,128,128]{3,2,1,0:T(8,128)(2,1)S(1)} %copy-done, bf16[64,2,128,128]{3,2,1,0:T(8,128)(2,1)S(1)} %broadcast_select_fusion.other, bf16[2048,128]{1,0:T(8,128)(2,1)S(1)} %pad_maximum_fusion.10.refs_0_, ...), custom_call_target="tpu_custom_call" | custom-call | flops 536870912 | bytes 4194304 | tf_op jit(solution)/shard_map/products/pallas_call | solution.py:55
  202.5 15.5 %collective-permute-start.75 = (bf16[4,64,128]{2,1,0:T(8,128)(2,1)S(1)}, bf16[4,64,128]{2,1,0:T(8,128)(2,1)S(1)}, u32[]{:S(2)}, u32[]{:S(2)}) collective-permute-start(bf16[4,64,128]{2,1,0:T(8,128)(2,1)S(1)} %bitcast.74), channel_id=1, source_target_pairs={{0,1},{1,0},{2,3},{3,2},{4,5},{5,4},{6,7},{7,6},{8,9},{9,8},{10,11... | collective-permute-start | bytes 196616 | tf_op jit(solution)/shard_map/ppermute | solution.py:23
  219.2 4.2 %collective-permute-start.76 = (bf16[4,64,128]{2,1,0:T(8,128)(2,1)S(1)}, bf16[4,64,128]{2,1,0:T(8,128)(2,1)S(1)}, u32[]{:S(2)}, u32[]{:S(2)}) collective-permute-start(bf16[4,64,128]{2,1,0:T(8,128)(2,1)S(1)} %bitcast.75), channel_id=1, source_target_pairs={{0,1},{1,0},{2,3},{3,2},{4,5},{5,4},{6,7},{7,6},{8,9},{9,8},{10,11... | collective-permute-start | bytes 196616 | tf_op jit(solution)/shard_map/ppermute | solution.py:23
  226.4 3.8 %collective-permute-done.70 = bf16[1024,128]{1,0:T(8,128)(2,1)S(1)} collective-permute-done((bf16[1024,128]{1,0:T(8,128)(2,1)S(1)}, bf16[1024,128]{1,0:T(8,128)(2,1)S(1)}, u32[]{:S(2)}, u32[]{:S(2)}) %collective-permute-start.70) | collective-permute-done | bytes 262176 | tf_op jit(solution)/shard_map/ppermute | solution.py:128
  234.2 3.0 %collective-permute-done.72 = bf16[512,128]{1,0:T(8,128)(2,1)S(1)} collective-permute-done((bf16[512,128]{1,0:T(8,128)(2,1)S(1)}, bf16[512,128]{1,0:T(8,128)(2,1)S(1)}, u32[]{:S(2)}, u32[]{:S(2)}) %collective-permute-start.72) | collective-permute-done | bytes 131104 | tf_op jit(solution)/shard_map/ppermute | solution.py:23
  238.6 3.0 %collective-permute-start.78 = (bf16[4,64,128]{2,1,0:T(8,128)(2,1)S(1)}, bf16[4,64,128]{2,1,0:T(8,128)(2,1)S(1)}, u32[]{:S(2)}, u32[]{:S(2)}) collective-permute-start(bf16[4,64,128]{2,1,0:T(8,128)(2,1)S(1)} %bitcast.77), channel_id=1, source_target_pairs={{0,1},{1,0},{2,3},{3,2},{4,5},{5,4},{6,7},{7,6},{8,9},{9,8},{10,11... | collective-permute-start | bytes 196616 | tf_op jit(solution)/shard_map/ppermute | solution.py:23
  (271 shorter events, 133.2 us)
Async XLA Ops:
  3.9 27.6 %collective-permute-start.3 = (bf16[64,2,128,128]{3,2,1,0:T(8,128)(2,1)}, bf16[64,2,128,128]{3,2,1,0:T(8,128)(2,1)}, u32[]{:S(2)}, u32[]{:S(2)}) collective-permute-start(bf16[64,2,128,128]{3,2,1,0:T(8,128)(2,1)} %bitcast.53), channel_id=1, source_target_pairs={{0,1},{1,0},{2,3},{3,2},{4,5},{5,4},{6,7},{7,6},{8,9},{9,8},{10,11... | collective-permute-start | bytes 12582920 | tf_op jit(solution)/shard_map/ppermute | solution.py:23
  5.7 15.3 %collective-permute-start.5 = (bf16[512,128]{1,0:T(8,128)(2,1)S(1)}, bf16[512,128]{1,0:T(8,128)(2,1)S(1)}, u32[]{:S(2)}, u32[]{:S(2)}) collective-permute-start(bf16[512,128]{1,0:T(8,128)(2,1)S(1)} %bitcast.61), channel_id=1, source_target_pairs={{0,64},{64,0},{1,65},{65,1},{2,66},{66,2},{3,67},{67,3},{4,68},{68... | collective-permute-start | bytes 393224 | tf_op jit(solution)/shard_map/ppermute | solution.py:23
  9.4 14.0 %collective-permute-start.4 = (bf16[1024,128]{1,0:T(8,128)(2,1)S(1)}, bf16[1024,128]{1,0:T(8,128)(2,1)S(1)}, u32[]{:S(2)}, u32[]{:S(2)}) collective-permute-start(bf16[1024,128]{1,0:T(8,128)(2,1)S(1)} %pad_maximum_fusion.12), channel_id=1, source_target_pairs={{0,16},{1,49},{16,0},{17,33},{32,48},{33,17},{48,32},{49,1},{2,18}... | collective-permute-start | bytes 786440 | tf_op jit(solution)/shard_map/ppermute | solution.py:122
  23.4 10.9 %collective-permute-start.6 = (bf16[2048,128]{1,0:T(8,128)(2,1)S(1)}, bf16[2048,128]{1,0:T(8,128)(2,1)S(1)}, u32[]{:S(2)}, u32[]{:S(2)}) collective-permute-start(bf16[2048,128]{1,0:T(8,128)(2,1)S(1)} %pad_maximum_fusion.refs_0_), channel_id=1, source_target_pairs={{0,48},{1,17},{16,32},{17,1},{32,16},{33,49},{48,0},{49,33},{2,50}... | collective-permute-start | bytes 1572872 | tf_op jit(solution)/shard_map/ppermute | solution.py:124
  29.1 13.4 %collective-permute-start.12 = (bf16[2048,128]{1,0:T(8,128)(2,1)S(1)}, bf16[2048,128]{1,0:T(8,128)(2,1)S(1)}, u32[]{:S(2)}, u32[]{:S(2)}) collective-permute-start(bf16[2048,128]{1,0:T(8,128)(2,1)S(1)} %pad_maximum_fusion.1.refs_0_), channel_id=1, source_target_pairs={{0,48},{1,17},{16,32},{17,1},{32,16},{33,49},{48,0},{49,33},{2,50}... | collective-permute-start | bytes 1572872 | tf_op jit(solution)/shard_map/ppermute | solution.py:124
  29.2 12.6 %collective-permute-start.13 = (bf16[1024,128]{1,0:T(8,128)(2,1)S(1)}, bf16[1024,128]{1,0:T(8,128)(2,1)S(1)}, u32[]{:S(2)}, u32[]{:S(2)}) collective-permute-start(bf16[1024,128]{1,0:T(8,128)(2,1)S(1)} %pad_maximum_fusion.14), channel_id=1, source_target_pairs={{0,16},{1,49},{16,0},{17,33},{32,48},{33,17},{48,32},{49,1},{2,18}... | collective-permute-start | bytes 786440 | tf_op jit(solution)/shard_map/ppermute | solution.py:122
  47.1 13.4 %collective-permute-start.18 = (bf16[2048,128]{1,0:T(8,128)(2,1)S(1)}, bf16[2048,128]{1,0:T(8,128)(2,1)S(1)}, u32[]{:S(2)}, u32[]{:S(2)}) collective-permute-start(bf16[2048,128]{1,0:T(8,128)(2,1)S(1)} %slice.398), channel_id=1, source_target_pairs={{0,12},{1,5},{4,8},{5,1},{8,4},{9,13},{12,0},{13,9},{2,14},{3,7},{... | collective-permute-start | bytes 1572872 | tf_op jit(solution)/shard_map/ppermute | solution.py:126
  50.9 12.8 %collective-permute-start.17 = (bf16[2048,128]{1,0:T(8,128)(2,1)S(1)}, bf16[2048,128]{1,0:T(8,128)(2,1)S(1)}, u32[]{:S(2)}, u32[]{:S(2)}) collective-permute-start(bf16[2048,128]{1,0:T(8,128)(2,1)S(1)} %pad_maximum_fusion.2.refs_0_), channel_id=1, source_target_pairs={{0,48},{1,17},{16,32},{17,1},{32,16},{33,49},{48,0},{49,33},{2,50}... | collective-permute-start | bytes 1572872 | tf_op jit(solution)/shard_map/ppermute | solution.py:124
  57.1 13.7 %collective-permute-start.20 = (bf16[2048,128]{1,0:T(8,128)(2,1)S(1)}, bf16[2048,128]{1,0:T(8,128)(2,1)S(1)}, u32[]{:S(2)}, u32[]{:S(2)}) collective-permute-start(bf16[2048,128]{1,0:T(8,128)(2,1)S(1)} %slice.401), channel_id=1, source_target_pairs={{0,12},{1,5},{4,8},{5,1},{8,4},{9,13},{12,0},{13,9},{2,14},{3,7},{... | collective-permute-start | bytes 1572872 | tf_op jit(solution)/shard_map/ppermute | solution.py:126
  57.7 10.7 %collective-permute-start.16 = (bf16[512,128]{1,0:T(8,128)(2,1)S(1)}, bf16[512,128]{1,0:T(8,128)(2,1)S(1)}, u32[]{:S(2)}, u32[]{:S(2)}) collective-permute-start(bf16[512,128]{1,0:T(8,128)(2,1)S(1)} %add_convert_fusion.27), channel_id=1, source_target_pairs={{0,2},{2,0},{1,3},{3,1},{4,6},{6,4},{5,7},{7,5},{8,10},{10,8},{9,1... | collective-permute-start | bytes 393224 | tf_op jit(solution)/shard_map/ppermute | solution.py:23
  73.7 11.9 %collective-permute-start.22 = (bf16[1024,128]{1,0:T(8,128)(2,1)S(1)}, bf16[1024,128]{1,0:T(8,128)(2,1)S(1)}, u32[]{:S(2)}, u32[]{:S(2)}) collective-permute-start(bf16[1024,128]{1,0:T(8,128)(2,1)S(1)} %pad_maximum_fusion.16), channel_id=1, source_target_pairs={{0,16},{1,49},{16,0},{17,33},{32,48},{33,17},{48,32},{49,1},{2,18}... | collective-permute-start | bytes 786440 | tf_op jit(solution)/shard_map/ppermute | solution.py:122
  89.2 11.1 %collective-permute-start.33 = (bf16[512,128]{1,0:T(8,128)(2,1)S(1)}, bf16[512,128]{1,0:T(8,128)(2,1)S(1)}, u32[]{:S(2)}, u32[]{:S(2)}) collective-permute-start(bf16[512,128]{1,0:T(8,128)(2,1)S(1)} %add_convert_fusion.20), channel_id=1, source_target_pairs={{0,64},{64,0},{1,65},{65,1},{2,66},{66,2},{3,67},{67,3},{4,68},{68... | collective-permute-start | bytes 393224 | tf_op jit(solution)/shard_map/ppermute | solution.py:23
  90.7 11.8 %collective-permute-start.36 = (bf16[2048,128]{1,0:T(8,128)(2,1)S(1)}, bf16[2048,128]{1,0:T(8,128)(2,1)S(1)}, u32[]{:S(2)}, u32[]{:S(2)}) collective-permute-start(bf16[2048,128]{1,0:T(8,128)(2,1)S(1)} %pad_maximum_fusion.5.refs_0_), channel_id=1, source_target_pairs={{0,48},{1,17},{16,32},{17,1},{32,16},{33,49},{48,0},{49,33},{2,50}... | collective-permute-start | bytes 1572872 | tf_op jit(solution)/shard_map/ppermute | solution.py:124
  115.4 12.6 %collective-permute-start.43 = (bf16[2048,128]{1,0:T(8,128)(2,1)S(1)}, bf16[2048,128]{1,0:T(8,128)(2,1)S(1)}, u32[]{:S(2)}, u32[]{:S(2)}) collective-permute-start(bf16[2048,128]{1,0:T(8,128)(2,1)S(1)} %pad_maximum_fusion.7.refs_0_), channel_id=1, source_target_pairs={{0,48},{1,17},{16,32},{17,1},{32,16},{33,49},{48,0},{49,33},{2,50}... | collective-permute-start | bytes 1572872 | tf_op jit(solution)/shard_map/ppermute | solution.py:124
  126.2 12.4 %collective-permute-start.46 = (bf16[2048,128]{1,0:T(8,128)(2,1)S(1)}, bf16[2048,128]{1,0:T(8,128)(2,1)S(1)}, u32[]{:S(2)}, u32[]{:S(2)}) collective-permute-start(bf16[2048,128]{1,0:T(8,128)(2,1)S(1)} %slice.443), channel_id=1, source_target_pairs={{0,12},{1,5},{4,8},{5,1},{8,4},{9,13},{12,0},{13,9},{2,14},{3,7},{... | collective-permute-start | bytes 1572872 | tf_op jit(solution)/shard_map/ppermute | solution.py:126
  150.9 12.4 %collective-permute-start.51 = (bf16[2048,128]{1,0:T(8,128)(2,1)S(1)}, bf16[2048,128]{1,0:T(8,128)(2,1)S(1)}, u32[]{:S(2)}, u32[]{:S(2)}) collective-permute-start(bf16[2048,128]{1,0:T(8,128)(2,1)S(1)} %pad_maximum_fusion.8.refs_0_), channel_id=1, source_target_pairs={{0,48},{1,17},{16,32},{17,1},{32,16},{33,49},{48,0},{49,33},{2,50}... | collective-permute-start | bytes 1572872 | tf_op jit(solution)/shard_map/ppermute | solution.py:124
  156.2 14.4 %collective-permute-start.60 = (bf16[2048,128]{1,0:T(8,128)(2,1)S(1)}, bf16[2048,128]{1,0:T(8,128)(2,1)S(1)}, u32[]{:S(2)}, u32[]{:S(2)}) collective-permute-start(bf16[2048,128]{1,0:T(8,128)(2,1)S(1)} %pad_maximum_fusion.9.refs_0_), channel_id=1, source_target_pairs={{0,48},{1,17},{16,32},{17,1},{32,16},{33,49},{48,0},{49,33},{2,50}... | collective-permute-start | bytes 1572872 | tf_op jit(solution)/shard_map/ppermute | solution.py:124
  169.8 11.2 %collective-permute-start.64 = (bf16[2048,128]{1,0:T(8,128)(2,1)S(1)}, bf16[2048,128]{1,0:T(8,128)(2,1)S(1)}, u32[]{:S(2)}, u32[]{:S(2)}) collective-permute-start(bf16[2048,128]{1,0:T(8,128)(2,1)S(1)} %pad_maximum_fusion.11.refs_0_), channel_id=1, source_target_pairs={{0,48},{1,17},{16,32},{17,1},{32,16},{33,49},{48,0},{49,33},{2,50}... | collective-permute-start | bytes 1572872 | tf_op jit(solution)/shard_map/ppermute | solution.py:124
  178.4 11.2 %collective-permute-start.66 = (bf16[2048,128]{1,0:T(8,128)(2,1)S(1)}, bf16[2048,128]{1,0:T(8,128)(2,1)S(1)}, u32[]{:S(2)}, u32[]{:S(2)}) collective-permute-start(bf16[2048,128]{1,0:T(8,128)(2,1)S(1)} %pad_maximum_fusion.10.refs_0_), channel_id=1, source_target_pairs={{0,48},{1,17},{16,32},{17,1},{32,16},{33,49},{48,0},{49,33},{2,50}... | collective-permute-start | bytes 1572872 | tf_op jit(solution)/shard_map/ppermute | solution.py:124
  178.6 15.6 %collective-permute-start.62 = (bf16[1024,128]{1,0:T(8,128)(2,1)S(1)}, bf16[1024,128]{1,0:T(8,128)(2,1)S(1)}, u32[]{:S(2)}, u32[]{:S(2)}) collective-permute-start(bf16[1024,128]{1,0:T(8,128)(2,1)S(1)} %add_convert_fusion.3), channel_id=1, source_target_pairs={{0,4},{1,13},{4,0},{5,9},{8,12},{9,5},{12,8},{13,1},{2,6},{3,15},{... | collective-permute-start | bytes 786440 | tf_op jit(solution)/shard_map/ppermute | solution.py:128
  198.7 24.7 %collective-permute-start.69 = (bf16[2048,128]{1,0:T(8,128)(2,1)S(1)}, bf16[2048,128]{1,0:T(8,128)(2,1)S(1)}, u32[]{:S(2)}, u32[]{:S(2)}) collective-permute-start(bf16[2048,128]{1,0:T(8,128)(2,1)S(1)} %slice.483), channel_id=1, source_target_pairs={{0,12},{1,5},{4,8},{5,1},{8,4},{9,13},{12,0},{13,9},{2,14},{3,7},{... | collective-permute-start | bytes 1572872 | tf_op jit(solution)/shard_map/ppermute | solution.py:126
  198.8 25.8 %collective-permute-start.71 = (bf16[2048,128]{1,0:T(8,128)(2,1)S(1)}, bf16[2048,128]{1,0:T(8,128)(2,1)S(1)}, u32[]{:S(2)}, u32[]{:S(2)}) collective-permute-start(bf16[2048,128]{1,0:T(8,128)(2,1)S(1)} %slice.492), channel_id=1, source_target_pairs={{0,12},{1,5},{4,8},{5,1},{8,4},{9,13},{12,0},{13,9},{2,14},{3,7},{... | collective-permute-start | bytes 1572872 | tf_op jit(solution)/shard_map/ppermute | solution.py:126
  200.3 17.7 %collective-permute-start.68 = (bf16[512,128]{1,0:T(8,128)(2,1)}, bf16[512,128]{1,0:T(8,128)(2,1)S(1)}, u32[]{:S(2)}, u32[]{:S(2)}) collective-permute-start(bf16[512,128]{1,0:T(8,128)(2,1)} %add_convert_fusion.14), channel_id=1, source_target_pairs={{0,2},{2,0},{1,3},{3,1},{4,6},{6,4},{5,7},{7,5},{8,10},{10,8},{9,1... | collective-permute-start | bytes 393224 | tf_op jit(solution)/shard_map/ppermute | solution.py:23
  202.5 22.1 %collective-permute-start.75 = (bf16[4,64,128]{2,1,0:T(8,128)(2,1)S(1)}, bf16[4,64,128]{2,1,0:T(8,128)(2,1)S(1)}, u32[]{:S(2)}, u32[]{:S(2)}) collective-permute-start(bf16[4,64,128]{2,1,0:T(8,128)(2,1)S(1)} %bitcast.74), channel_id=1, source_target_pairs={{0,1},{1,0},{2,3},{3,2},{4,5},{5,4},{6,7},{7,6},{8,9},{9,8},{10,11... | collective-permute-start | bytes 196616 | tf_op jit(solution)/shard_map/ppermute | solution.py:23
  (62 other events, 483.3 us)
